TPU v7x, 32 devices: a whole 2x2x4 slice. The times are simulated.
32 devices in a mesh: dp: 4 (over y, x), seq: 8 (over z, core).
Axes of the slice: x: 2, y: 2, z: 4, core: 2. Of those that a mesh axis runs over, the one named last changes fastest.
Arguments:
- frames_in: bfloat16 [8, 16, 144, 1152], P('dp', 'seq'), may hold values from -36 to 36
- modulation: float32 [8, 6, 1152], P('dp'), may hold values from -3 to 3
- spatial_qkv: bfloat16 [1152, 3456], replicated, may hold values from -0.8249579 to 0.8249579
- spatial_out: bfloat16 [1152, 1152], replicated, may hold values from -0.1875 to 0.1875
- temporal_qkv: bfloat16 [1152, 3456], replicated, may hold values from -0.8249579 to 0.8249579
- temporal_out: bfloat16 [1152, 1152], replicated, may hold values from -0.1875 to 0.1875
- cotangent: bfloat16 [8, 16, 144, 1152], P('dp', 'seq'), may hold values from -6 to 6
Outputs:
- block_out: bfloat16 [8, 16, 144, 1152], P('dp', 'seq')
- grad_input: bfloat16 [8, 16, 144, 1152], P('dp', 'seq')
- grad_spatial_qkv: bfloat16 [1152, 3456], P(('dp', 'seq'))
- grad_spatial_out: bfloat16 [1152, 1152], P(('dp', 'seq'))
- grad_temporal_qkv: bfloat16 [1152, 3456], P(('dp', 'seq'))
- grad_temporal_out: bfloat16 [1152, 1152], P(('dp', 'seq'))
All inputs are finite; a program needn't handle non-finite values.
Results may differ from a plain program's by a relative error of at most 0.02.
Values may be sent and summed in bfloat16 or wider, within the bound.
No kernel may reach another device: no remote copies, remote signals or barrier semaphores. Data moves between devices by JAX's collectives and lax.ppermute only.
A program may use at most 192 MiB of HBM per device.

v0:
```python
import jax
import jax.numpy as jnp
from jax import lax
from jax.sharding import PartitionSpec as P

HEADS = 16
FRAMES = 16
PATCHES = 144


NORM_EPSILON = 1e-06


def shortened(x):

    def short(part):
        return part.astype(jnp.bfloat16) if part.dtype == jnp.float32 else part

    return jax.tree.map(short, x)


def heads_view(values):
    return values.reshape(values.shape[:-1] + (HEADS, values.shape[-1] // HEADS))


def attend(queries, key_in, value_in, attend_axis):
    factor = queries.shape[-1] ** (-0.5)
    if attend_axis == "space":
        scores = (
            jnp.einsum("vfpne,vfqne->vfnpq", queries, key_in, preferred_element_type=jnp.float32)
            * factor
        )
    else:
        scores = (
            jnp.einsum("vfpne,vgpne->vpnfg", queries, key_in, preferred_element_type=jnp.float32)
            * factor
        )
    softmax_out = jax.nn.softmax(scores, axis=-1)
    weights = softmax_out.astype(jnp.bfloat16)
    if attend_axis == "space":
        mixed_heads = jnp.einsum(
            "vfnpq,vfqne->vfpne", weights, value_in, preferred_element_type=jnp.float32
        )
    else:
        mixed_heads = jnp.einsum(
            "vpnfg,vgpne->vfpne", weights, value_in, preferred_element_type=jnp.float32
        )
    return (softmax_out, weights, mixed_heads)


def branch_forward(tokens_in, shift, scale, gate, w_qkv, w_out, attend_axis):
    values = tokens_in.astype(jnp.float32)
    row_mean = jnp.mean(values, -1, keepdims=True)
    centred = values - row_mean
    inverse = lax.rsqrt(jnp.mean(centred * centred, -1, keepdims=True) + NORM_EPSILON)
    normed = centred * inverse
    modded = (normed * (1.0 + scale) + shift).astype(jnp.bfloat16)
    packed = jnp.dot(modded, w_qkv, preferred_element_type=jnp.float32).astype(jnp.bfloat16)
    model_width = w_out.shape[0]
    queries = heads_view(packed[..., :model_width])
    key_in = heads_view(packed[..., model_width : 2 * model_width])
    value_in = heads_view(packed[..., 2 * model_width :])
    softmax_out, weights, mixed_heads = attend(queries, key_in, value_in, attend_axis)
    attended = mixed_heads.reshape(tokens_in.shape).astype(jnp.bfloat16)
    projected = jnp.dot(attended, w_out, preferred_element_type=jnp.float32)
    result = (values + gate * projected).astype(jnp.bfloat16)
    saved = (normed, inverse, modded, queries, key_in, value_in, softmax_out, weights, attended)
    return (result, saved)


def branch_backward(saved, scale, gate, w_qkv, w_out, attend_axis, upstream):
    normed, inverse, modded, queries, key_in, value_in, softmax_out, weights, attended = saved
    incoming = upstream.astype(jnp.float32)
    scaled_grad = (gate * incoming).astype(jnp.bfloat16)
    d_attended = jnp.dot(scaled_grad, w_out.T, preferred_element_type=jnp.float32).astype(
        jnp.bfloat16
    )
    d_heads = heads_view(d_attended)
    factor = queries.shape[-1] ** (-0.5)
    if attend_axis == "space":
        d_value = jnp.einsum(
            "vfnpq,vfpne->vfqne", weights, d_heads, preferred_element_type=jnp.float32
        )
        d_probs = jnp.einsum(
            "vfpne,vfqne->vfnpq", d_heads, value_in, preferred_element_type=jnp.float32
        )
    else:
        d_value = jnp.einsum(
            "vpnfg,vfpne->vgpne", weights, d_heads, preferred_element_type=jnp.float32
        )
        d_probs = jnp.einsum(
            "vfpne,vgpne->vpnfg", d_heads, value_in, preferred_element_type=jnp.float32
        )
    d_scores = (
        softmax_out * (d_probs - jnp.sum(softmax_out * d_probs, -1, keepdims=True)) * factor
    ).astype(jnp.bfloat16)
    if attend_axis == "space":
        d_query = jnp.einsum(
            "vfnpq,vfqne->vfpne", d_scores, key_in, preferred_element_type=jnp.float32
        )
        d_key = jnp.einsum(
            "vfnpq,vfpne->vfqne", d_scores, queries, preferred_element_type=jnp.float32
        )
    else:
        d_query = jnp.einsum(
            "vpnfg,vgpne->vfpne", d_scores, key_in, preferred_element_type=jnp.float32
        )
        d_key = jnp.einsum(
            "vpnfg,vfpne->vgpne", d_scores, queries, preferred_element_type=jnp.float32
        )
    shape_out = upstream.shape
    d_packed = jnp.concatenate(
        [d_query.reshape(shape_out), d_key.reshape(shape_out), d_value.reshape(shape_out)], -1
    ).astype(jnp.bfloat16)
    d_modded = jnp.dot(d_packed, w_qkv.T, preferred_element_type=jnp.float32)
    d_normed = d_modded * (1.0 + scale)
    d_tokens = inverse * (
        d_normed
        - jnp.mean(d_normed, -1, keepdims=True)
        - normed * jnp.mean(d_normed * normed, -1, keepdims=True)
    )
    result = (incoming + d_tokens).astype(jnp.bfloat16)
    return (result, ((modded, d_packed), (attended, scaled_grad)))


def weight_term(left_rows, right_rows, grad_scale):
    one_term = jnp.einsum(
        "vfpd,vfpc->dc", left_rows, right_rows, preferred_element_type=jnp.float32
    )
    return (one_term * grad_scale).astype(jnp.bfloat16)


def reduce_terms(weight_terms):
    data_count = lax.axis_size("dp")
    seq_count = lax.axis_size("seq")
    blocks = tuple(
        (
            piece.reshape(
                data_count, seq_count, piece.shape[0] // (data_count * seq_count), piece.shape[1]
            )
            for piece in weight_terms
        )
    )
    section_one = jax.tree.map(
        lambda part: part.astype(jnp.float32),
        lax.psum_scatter(shortened(blocks), "seq", scatter_dimension=1, tiled=True),
    )
    section_two = jax.tree.map(
        lambda part: part.astype(jnp.float32),
        lax.psum_scatter(shortened(section_one), "dp", scatter_dimension=0, tiled=True),
    )
    return tuple(
        (
            piece.reshape(piece.shape[2], piece.shape[3]).astype(jnp.bfloat16)
            for piece in section_two
        )
    )


def shards(frames_in, modulation, spatial_qkv, spatial_out, temporal_qkv, temporal_out, cotangent):
    mod_rows = modulation[:, :, None, None, :]
    middle, saved_space = branch_forward(
        frames_in, mod_rows[:, 0], mod_rows[:, 1], mod_rows[:, 2], spatial_qkv, spatial_out, "space"
    )
    by_position = lax.all_to_all(middle, "seq", split_axis=2, concat_axis=1, tiled=True)
    mixed_out, saved_time = branch_forward(
        by_position,
        mod_rows[:, 3],
        mod_rows[:, 4],
        mod_rows[:, 5],
        temporal_qkv,
        temporal_out,
        "time",
    )
    block_out = lax.all_to_all(mixed_out, "seq", split_axis=1, concat_axis=2, tiled=True)
    upstream = lax.all_to_all(cotangent, "seq", split_axis=2, concat_axis=1, tiled=True)
    d_position, time_terms = branch_backward(
        saved_time, mod_rows[:, 4], mod_rows[:, 5], temporal_qkv, temporal_out, "time", upstream
    )
    d_middle = lax.all_to_all(d_position, "seq", split_axis=1, concat_axis=2, tiled=True)
    grad_input, space_terms = branch_backward(
        saved_space, mod_rows[:, 1], mod_rows[:, 2], spatial_qkv, spatial_out, "space", d_middle
    )
    grad_scale = (frames_in.shape[0] * lax.axis_size("dp") * FRAMES * PATCHES) ** (-0.5)
    weight_terms = (
        weight_term(space_terms[0][0], space_terms[0][1], grad_scale),
        weight_term(space_terms[1][0], space_terms[1][1], grad_scale),
        weight_term(time_terms[0][0], time_terms[0][1], grad_scale),
        weight_term(time_terms[1][0], time_terms[1][1], grad_scale),
    )
    reduced = reduce_terms(weight_terms)
    return (block_out, grad_input, reduced[0], reduced[1], reduced[2], reduced[3])


def solution(mesh):
    return jax.shard_map(
        shards,
        mesh=mesh,
        in_specs=(
            P("dp", "seq", None, None),
            P("dp", None, None),
            P(),
            P(),
            P(),
            P(),
            P("dp", "seq", None, None),
        ),
        out_specs=(
            P("dp", "seq", None, None),
            P("dp", "seq", None, None),
            P(("dp", "seq"), None),
            P(("dp", "seq"), None),
            P(("dp", "seq"), None),
            P(("dp", "seq"), None),
        ),
        check_vma=False,
    )
```

profile of v0, /device:TPU:0, one launch (start us, length us, event | category | flops | bytes accessed | tf_op | source)
XLA Modules:
  0.0 1003.1 jit_solution(8212997057924618824)
XLA Ops:
  10.9 9.3 fusion.27
  26.2 6.1 reshape.183
  36.3 9.8 fusion.152
  46.1 5.8 fusion.118
  56.2 6.3 all-to-all-start
  65.9 29.3 %all-to-all-done = bf16[2,2,144,1152]{3,1,0,2:T(2,128)(2,1)} async-done(((bf16[2,2,144,1152]{3,1,0,2:T(2,128)(2,1)}), bf16[2,2,144,1152]{3,1,0,2:T(2,128)(2,1)}, u32[]{:S(2)}, u32[]{:S(2)}) %all-to-all-start) | async-done | bytes 1327136 | tf_op jit(solution)/shard_map/all_to_all | solution.py:165
  95.2 4.8 all-to-all-start.2
  111.2 21.5 %all-to-all-done.2 = bf16[2,2,144,1152]{3,1,0,2:T(2,128)(2,1)} async-done(((bf16[2,2,144,1152]{3,1,0,2:T(2,128)(2,1)}), bf16[2,2,144,1152]{3,1,0,2:T(2,128)(2,1)}, u32[]{:S(2)}, u32[]{:S(2)}) %all-to-all-start.2) | async-done | bytes 1327136 | tf_op jit(solution)/shard_map/all_to_all | solution.py:176
  144.0 6.4 reshape.230
  153.9 12.0 %fusion.22 = bf16[2,16,18,3456]{3,2,1,0:T(8,128)(2,1)S(1)} fusion(bf16[1152,3456]{1,0:T(8,128)(2,1)} %param.11, f32[2,16,18,1152]{3,2,1,0:T(8,128)} %bitcast.164, f32[2,1152]{1,0:T(2,128)S(1)} %get-tuple-element.51, f32[2,1152]{1,0:T(2,128)S(1)} %get-tuple-element.52, f32[2,16,18]{2,1,0:T(8,128)S(1)} %bitcast.187, f32[2,16,18]{2,1,0:T(8,128)S(1)} %bitcast.183), kind=kOutput, calls=%fused_computation.30 | convolution fusion | flops 4591779840 | bytes 14621184 | tf_op jit(solution)/shard_map/dot_general | solution.py:58
  168.3 6.4 reshape.228
  174.7 6.4 reshape.229
  181.1 6.4 reshape.227
  199.3 11.1 %convert_bitcast_fusion.2 = bf16[2,16,18,16,72]{4,1,3,2,0:T(8,128)(2,1)} fusion(f32[2,18,16,16,16]{3,4,2,1,0:T(8,128)} %fusion.87, bf16[2,16,18,16,72]{4,3,2,1,0:T(8,128)(2,1)} %reshape.229, f32[2,18,16,16,16]{3,4,2,1,0:T(8,128)} %get-tuple-element.59, f32[2,18,16,16]{3,2,1,0:T(8,128)S(1)} %get-tuple-element.58), kind=kOutput, calls=%fused_computation.84 | convolution fusion | flops 22938640 | bytes 3870720 | tf_op jit(solution)/shard_map/vpnfg,vgpne->vfpne/dot_general | solution.py:105
  210.4 11.1 %convert_bitcast_fusion.1 = bf16[2,16,18,16,72]{4,1,3,2,0:T(8,128)(2,1)} fusion(f32[2,18,16,16,16]{3,4,2,1,0:T(8,128)} %fusion.87, bf16[2,16,18,16,72]{4,3,2,1,0:T(8,128)(2,1)} %reshape.228, f32[2,18,16,16,16]{3,4,2,1,0:T(8,128)} %get-tuple-element.59, f32[2,18,16,16]{3,2,1,0:T(8,128)S(1)} %get-tuple-element.58), kind=kOutput, calls=%fused_computation.83 | convolution fusion | flops 22938640 | bytes 3870720 | tf_op jit(solution)/shard_map/vpnfg,vfpne->vgpne/dot_general | solution.py:108
  221.5 5.7 convert_bitcast_fusion
  227.2 4.3 convert_bitcast_fusion.3
  233.6 5.5 reshape.217
  242.7 5.5 reshape.216
  251.9 5.8 reshape.218
  263.2 12.6 %fusion.148 = (f32[2,16,18]{2,1,0:T(8,128)S(1)}, f32[2,16,18]{2,1,0:T(8,128)S(1)}, f32[2,16,18,1152]{3,2,1,0:T(8,128)}) fusion(f32[2,16,18]{2,1,0:T(8,128)S(1)} %bitcast.188, f32[2,16,18,1152]{3,2,1,0:T(8,128)S(1)} %bitcast.167, f32[2,16,18]{2,1,0:T(8,128)S(1)} %bitcast.184, f32[2,1152]{1,0:T(2,128)S(1)} %get-tuple-element.52, ...), kind=kOutput, calls=%fused_computation.157 | convolution fusion | flops 4590451712 | bytes 17270784 | tf_op jit(solution)/shard_map/dot_general | solution.py:115
  275.9 9.3 fusion.6
  287.3 4.8 convert_element_type.171
  292.1 4.8 add_convert_fusion
  299.4 4.3 all-to-all-start.3
  303.7 5.9 fusion.20
  309.5 5.1 reshape.200
  314.6 5.5 copy.392
  320.1 12.4 %reshape.199 = bf16[4,8,36,3456]{3,2,1,0:T(8,128)(2,1)} reshape(bf16[1152,3456]{1,0:T(8,128)(2,1)} %fusion.6) | data formatting | bytes 15925248 | tf_op jit(solution)/shard_map/reshape | solution.py:138
  332.5 8.4 copy.388
  350.6 4.0 copy.428
  354.7 7.7 fusion.123
  362.4 4.9 fusion.98
  367.3 17.2 %fusion.112 = bf16[2,2,16,72,144]{4,3,2,1,0:T(8,128)(2,1)} fusion(bf16[2,2,144,16,72]{2,4,3,1,0:T(8,128)(2,1)} %bitcast.177, f32[2,2,16,144,144]{3,4,2,1,0:T(8,128)} %fusion.98, f32[2,2,16,144,144]{3,4,2,1,0:T(8,128)} %get-tuple-element.57, f32[2,2,16,144]{3,2,1,0:T(8,128)S(1)} %copy-done.36), kind=kOutput, calls=%fused_computation.109 | convolution fusion | flops 201065616 | bytes 13307904 | tf_op jit(solution)/shard_map/vfnpq,vfqne->vfpne/dot_general | solution.py:98
  384.5 16.6 %fusion.115 = bf16[2,2,16,72,144]{4,3,2,1,0:T(8,128)(2,1)} fusion(bf16[2,2,144,16,72]{2,4,3,1,0:T(8,128)(2,1)} %bitcast.179, f32[2,2,16,144,144]{3,4,2,1,0:T(8,128)} %fusion.98, f32[2,2,16,144,144]{3,4,2,1,0:T(8,128)} %get-tuple-element.57, f32[2,2,16,144]{3,2,1,0:T(8,128)S(1)} %copy-done.36), kind=kOutput, calls=%fused_computation.110 | convolution fusion | flops 201065616 | bytes 13307904 | tf_op jit(solution)/shard_map/vfnpq,vfpne->vfqne/dot_general | solution.py:101
  401.1 5.1 reshape.198
  406.2 5.4 copy.384
  419.5 4.4 copy.374
  424.0 12.5 %fusion.7 = bf16[1152,3456]{1,0:T(8,128)(2,1)} fusion(bf16[2,2,144,1152]{3,2,1,0:T(8,128)(2,1)} %copy.376, bf16[2,2,144,1152]{3,2,1,0:T(8,128)(2,1)} %copy.375, bf16[2,2,144,1152]{3,2,1,0:T(8,128)(2,1)} %copy.374, bf16[2,2,144,1152]{3,2,1,0:T(8,128)(2,1)} %param.7, f32[2,1152]{1,0:T(2,128)S(1)} %copy-done.28, f32[2,1152]{1,0:T(2,128)S(1)} %copy-done.26, ...), kind=kOutput, calls=%fused_computation.9 | convolution fusion | flops 4610359296 | bytes 13294080 | tf_op jit(solution)/shard_map/vfpd,vfpc->dc/dot_general | solution.py:127
  436.5 12.4 %reshape.197 = bf16[4,8,36,3456]{3,2,1,0:T(8,128)(2,1)} reshape(bf16[1152,3456]{1,0:T(8,128)(2,1)} %fusion.7) | data formatting | bytes 15925248 | tf_op jit(solution)/shard_map/reshape | solution.py:138
  448.9 8.4 copy.380
  458.6 419.0 %all-reduce.11.cloned.1.call-done = (bf16[4,8,36,3456]{3,0,2,1:T(4,128)(2,1)}, bf16[4,8,36,1152]{3,0,2,1:T(4,128)(2,1)}, bf16[4,8,36,3456]{3,0,2,1:T(4,128)(2,1)}, bf16[4,8,36,1152]{3,0,2,1:T(4,128)(2,1)}) async-done(((bf16[4,8,36,3456]{3,0,2,1:T(4,128)(2,1)}, bf16[4,8,36,1152]{3,0,2,1:T(4,128)(2,1)}, bf16[4,8,36,3456]{3,0,2,1:T(4,128)(2,1)}, bf16[4,8,36,1152]{3,0,2,1:T(4,128)(2,1)}), ...) | async-done | bytes 21233680
  880.1 6.0 fusion.54
  888.6 4.3 all-to-all-start.1
  899.1 26.3 %all-to-all-done.1 = bf16[2,16,18,1152]{3,0,2,1:T(2,128)(2,1)} async-done(((bf16[2,16,18,1152]{3,0,2,1:T(2,128)(2,1)}), bf16[2,16,18,1152]{3,0,2,1:T(2,128)(2,1)}, u32[]{:S(2)}, u32[]{:S(2)}) %all-to-all-start.1) | async-done | bytes 1327136 | tf_op jit(solution)/shard_map/all_to_all | solution.py:175
  932.3 10.4 %fusion.149 = (f32[2,2,144]{2,1,0:T(2,128)S(1)}, f32[2,2,144]{2,1,0:T(2,128)S(1)}, f32[2,2,144,1152]{3,2,1,0:T(8,128)S(1)}) fusion(f32[2,2,144]{2,1,0:T(2,128)S(1)} %copy-done.24, f32[2,2,144]{2,1,0:T(2,128)S(1)} %copy-done.20, bf16[2,2,144,1152]{3,2,1,0:T(8,128)(2,1)} %param.7, f32[2,1152]{1,0:T(2,128)S(1)} %copy-done.26, bf16[1152,3456]{1,0:T(8,128)(2,1)} %param.9, ...), kind=kOutput, calls=%fused_computation.158 | convolution fusion | flops 4603059200 | bytes 15943680 | tf_op jit(solution)/shard_map/dot_general | solution.py:115
  944.7 20.0 %reduce-scatter.13.cloned.1.call-done = bf16[1,1,36,3456]{3,2,1,0:T(8,128)(2,1)} async-done(((bf16[4,1,36,3456]{3,2,1,0:T(8,128)(2,1)}), bf16[1,1,36,3456]{3,2,1,0:T(8,128)(2,1)}) %reduce-scatter.13.cloned.1.call-update) | async-done | bytes 248848
  964.6 31.8 %reduce-scatter.17.cloned.1.call-done = bf16[1,1,36,3456]{3,2,1,0:T(8,128)(2,1)} async-done(((bf16[4,1,36,3456]{3,2,1,0:T(8,128)(2,1)}), bf16[1,1,36,3456]{3,2,1,0:T(8,128)(2,1)}) %reduce-scatter.17.cloned.1.call-update) | async-done | bytes 248848
  (148 shorter events, 119.7 us)
Async XLA Ops:
  7.2 44.8 %copy-start = (bf16[1152,1152]{1,0:T(8,128)(2,1)S(1)}, bf16[1152,1152]{1,0:T(8,128)(2,1)}, u32[]{:S(2)}) copy-start(bf16[1152,1152]{1,0:T(8,128)(2,1)} %param.10) | copy-start | bytes 7962628
  7.2 3.7 copy-start.3
  7.2 3.6 copy-start.18
  9.0 11.3 %copy-start.19 = (f32[2,2,144]{2,1,0:T(2,128)}, f32[2,2,144]{2,1,0:T(2,128)S(1)}, u32[]{:S(2)}) copy-start(f32[2,2,144]{2,1,0:T(2,128)S(1)} %broadcast_multiply_fusion.5) | copy-start | bytes 6916
  10.8 9.5 copy-start.23
  10.9 9.4 copy-start.25
  10.9 9.4 copy-start.27
  10.9 41.1 %copy-start.29 = (f32[2,1152]{1,0:T(2,128)}, f32[2,1152]{1,0:T(2,128)S(1)}, u32[]{:S(2)}) copy-start(f32[2,1152]{1,0:T(2,128)S(1)} %get-tuple-element.55) | copy-start | bytes 27652
  10.9 124.9 %copy-start.21 = (f32[2,1152]{1,0:T(2,128)}, f32[2,1152]{1,0:T(2,128)S(1)}, u32[]{:S(2)}) copy-start(f32[2,1152]{1,0:T(2,128)S(1)} %get-tuple-element.50) | copy-start | bytes 27652
  46.1 5.9 copy-start.35
  46.1 5.9 copy-start.4
  52.0 2.2 copy-start.32
  56.2 39.0 %all-to-all-start = ((bf16[2,2,144,1152]{3,1,0,2:T(2,128)(2,1)}), bf16[2,2,144,1152]{3,1,0,2:T(2,128)(2,1)}, u32[]{:S(2)}, u32[]{:S(2)}) async-start(bf16[2,2,144,1152]{3,1,0,2:T(2,128)(2,1)} %copy.326), calls=%async_computation | async-start | bytes 2654208 | tf_op jit(solution)/shard_map/all_to_all | solution.py:165
  95.2 37.4 %all-to-all-start.2 = ((bf16[2,2,144,1152]{3,1,0,2:T(2,128)(2,1)}), bf16[2,2,144,1152]{3,1,0,2:T(2,128)(2,1)}, u32[]{:S(2)}, u32[]{:S(2)}) async-start(bf16[2,2,144,1152]{3,1,0,2:T(2,128)(2,1)} %copy.346), calls=%async_computation.2 | async-start | bytes 2654208 | tf_op jit(solution)/shard_map/all_to_all | solution.py:176
  135.8 1.9 copy-start.1
  137.7 2.4 copy-start.31
  138.0 1.2 copy-start.17
  191.4 3.9 copy-start.10
  191.5 3.9 copy-start.11
  221.5 5.7 copy-start.12
  227.2 4.3 copy-start.16
  257.7 2.0 copy-start.13
  259.8 1.5 copy-start.14
  261.2 2.0 copy-start.2
  275.9 9.3 copy-start.15
  299.4 41.6 %all-to-all-start.3 = ((bf16[2,16,18,1152]{3,0,2,1:T(2,128)(2,1)}), bf16[2,16,18,1152]{3,0,2,1:T(2,128)(2,1)}, u32[]{:S(2)}, u32[]{:S(2)}) async-start(bf16[2,16,18,1152]{3,0,2,1:T(2,128)(2,1)} %copy.363), calls=%async_computation.3 | async-start | bytes 2654208 | tf_op jit(solution)/shard_map/all_to_all | solution.py:180
  303.6 574.0 %all-reduce.11.cloned.1.call-start = ((), (), s32[]{:S(2)}) async-start(), calls=%async_computation.12 | async-start | bytes 42467328
  340.9 2.5 copy-start.30
  340.9 2.5 copy-start.33
  343.4 4.0 copy-start.6
  350.6 4.1 copy-start.36
  354.7 7.7 copy-start.8
  354.7 7.7 copy-start.9
  419.5 4.4 copy-start.20
  419.5 4.4 copy-start.24
  419.5 4.4 copy-start.26
  419.5 4.5 copy-start.28
  457.3 0.7 copy-start.34
  457.3 422.8 %copy-start.22 = (f32[2,1152]{1,0:T(2,128)S(1)}, f32[2,1152]{1,0:T(2,128)}, u32[]{:S(2)}) copy-start(f32[2,1152]{1,0:T(2,128)} %copy-done.21) | copy-start | bytes 27652
  457.3 487.3 %reduce-scatter.15.cloned.1.call-start = ((), (), s32[]{:S(2)}) async-start(), calls=%async_computation.9 | async-start | bytes 460800
  888.6 36.8 %all-to-all-start.1 = ((bf16[2,16,18,1152]{3,0,2,1:T(2,128)(2,1)}), bf16[2,16,18,1152]{3,0,2,1:T(2,128)(2,1)}, u32[]{:S(2)}, u32[]{:S(2)}) async-start(bf16[2,16,18,1152]{3,0,2,1:T(2,128)(2,1)} %copy.344), calls=%async_computation.1 | async-start | bytes 2654208 | tf_op jit(solution)/shard_map/all_to_all | solution.py:175
  892.8 51.8 %reduce-scatter.19.cloned.1.call-start = ((), (), s32[]{:S(2)}) async-start(), calls=%async_computation.11 | async-start | bytes 460800
  895.5 69.2 %reduce-scatter.13.cloned.1.call-start = ((), (), s32[]{:S(2)}) async-start(), calls=%async_computation.8 | async-start | bytes 1382400
  899.1 97.3 %reduce-scatter.17.cloned.1.call-start = ((), (), s32[]{:S(2)}) async-start(), calls=%async_computation.10 | async-start | bytes 1382400
  932.3 10.4 %copy-start.5 = (bf16[2,2,144,1152]{3,2,1,0:T(8,128)(2,1)S(1)}, bf16[2,2,144,1152]{3,2,1,0:T(8,128)(2,1)}, u32[]{:S(2)}) copy-start(bf16[2,2,144,1152]{3,2,1,0:T(8,128)(2,1)} %param.7) | copy-start | bytes 3981316
  932.3 10.4 %copy-start.7 = (f32[2,8,2,18,1152]{4,2,3,1,0:T(2,128)S(1)}, f32[2,8,2,18,1152]{4,2,3,1,0:T(2,128)}, u32[]{:S(2)}) copy-start(f32[2,8,2,18,1152]{4,2,3,1,0:T(2,128)} %copy-done.6) | copy-start | bytes 7962628
Sparse Core Ops, SparseCore 0:
  457.5 420.0 all-reduce.10
  881.2 23.9 reduce-scatter.14
  908.7 23.8 reduce-scatter.18
  936.3 28.3 reduce-scatter.12
  968.0 28.3 reduce-scatter.16
where the time goes:
time: 1010 us; the launch traced here: 1000 us
  waiting for transfers between devices  548 us (54%)
  local copies, waits for them, and re-layouts  204 us (20%)
  matrix products  193 us (19%)
  other arithmetic  23.4 us (2%)
  starting transfers between devices  20 us (2%)
  between operations  14.6 us (1%)
    unnamed x10, waiting for transfers between devices  471 us
    reshape x8, local copies, waits for them, and re-layouts, reduce_terms(): piece.reshape(data_count, seq_count, piece.shape[0] // (data_count * seq_...  62.7 us
    reshape x8, local copies, waits for them, and re-layouts, heads_view(): values.reshape(values.shape[:-1] + (HEADS, values.shape[-1] // HEADS))  43.5 us
    dot_general x4, matrix products, weight_term(): jnp.einsum('vfpd,vfpc->dc', left_rows, right_rows, preferred_element_type...  31.6 us
    all_to_all x1, waiting for transfers between devices, shards(): lax.all_to_all(middle, 'seq', split_axis=2, concat_axis=1, tiled=True)  29.3 us
    all_to_all x1, waiting for transfers between devices, shards(): lax.all_to_all(mixed_out, 'seq', split_axis=1, concat_axis=2, tiled=True)  26.3 us
    dot_general x2, matrix products, branch_backward(): d_modded = jnp.dot(d_packed, w_qkv.T, preferred_element_type=jnp.float32)  23 us
    unnamed x83, local copies, waits for them, and re-layouts  22.9 us
  transfers between devices with their start and end apart: 9, of which 6 were waited for; matrix products, arithmetic and copies ran while one was open for 9% of the time, Pallas kernels for 0%

commit v1 on v0

v1 whole, which is shorter than its diff:
```python
import functools

import jax
import jax.numpy as jnp
import numpy as np
from jax import lax
from jax.experimental import pallas as pl
from jax.experimental.pallas import tpu as pltpu
from jax.sharding import PartitionSpec as P

HEADS = 16
NORM_EPSILON = 1e-06
MASKED = -1e30
LOG2_E = 1.4426950408889634
MIB = 1024 * 1024
F32 = jnp.float32
BF16 = jnp.bfloat16

NN = (((1,), (0,)), ((), ()))
NT = (((1,), (1,)), ((), ()))
TN = (((0,), (0,)), ((), ()))


def dot(left, right, dims=NN):
    return lax.dot_general(left, right, dims, preferred_element_type=F32)


SPACES = {"v": pltpu.VMEM, "s": pltpu.SMEM, "a": pl.ANY}


def call(name, us, body, ins, out_shape, outs, scratch=()):
    def run(*operands, deps=()):
        return pl.pallas_call(
            body,
            out_shape=out_shape,
            in_specs=[pl.BlockSpec(memory_space=SPACES[s]) for s in ins + "a" * len(deps)],
            out_specs=(
                tuple(pl.BlockSpec(memory_space=SPACES[s]) for s in outs)
                if isinstance(out_shape, tuple)
                else pl.BlockSpec(memory_space=SPACES[outs])
            ),
            scratch_shapes=list(scratch),
            compiler_params=pltpu.CompilerParams(vmem_limit_bytes=(56 if us > 4 else 16) * MIB),
            cost_estimate=pl.CostEstimate(
                flops=int(us * 1e9), transcendentals=0, bytes_accessed=int(us * 1e6)
            ),
            name=name,
        )(*operands, *deps)

    return run


def shaped(*shape, dtype=BF16):
    return jax.ShapeDtypeStruct(shape, dtype)


def norm_stats(values):
    mean = jnp.mean(values, -1, keepdims=True)
    centred = values - mean
    inverse = lax.rsqrt(jnp.mean(centred * centred, -1, keepdims=True) + NORM_EPSILON)
    return centred * inverse, inverse


def norm_backward(d_modded, normed, inverse, scale):
    e = d_modded * (1.0 + scale)
    return inverse * (
        e
        - jnp.mean(e, -1, keepdims=True)
        - normed * jnp.mean(e * normed, -1, keepdims=True)
    )


def pair_windows(width):
    size = 2 * width // HEADS
    found = []
    for pair in range(HEADS // 2):
        start = pair * size // 128 * 128
        offset = pair * size - start
        found.append((start, 128 * pl.cdiv(offset + size, 128), offset))
    return found


def pair_masks(rows, span, offset, size):
    lane = lax.broadcasted_iota(jnp.int32, (rows, span), 1)
    first = (lane >= offset) & (lane < offset + size)
    both = (lane >= offset) & (lane < offset + 2 * size)
    return first, both


def two_heads(values, first, both):
    zero = jnp.zeros_like(values)
    return jnp.concatenate(
        [jnp.where(first, values, zero), jnp.where(both & ~first, values, zero)], 0
    )


def per_query(by_key, other, first):
    out = dot(by_key, other, TN)
    rows = out.shape[0] // 2
    return jnp.where(first, out[:rows], out[rows:])


def probs_by_key(queries, key, factor, keep):
    scores = dot(key, queries, NT)
    if keep is not None:
        scores = jnp.where(keep, scores, MASKED)
    raised = jnp.exp2((scores - jnp.max(scores, 0, keepdims=True)) * (factor * LOG2_E))
    return raised * (1.0 / jnp.sum(raised, 0, keepdims=True))


def put(ref, rows, start, both, value):
    at = (pl.ds(rows, both.shape[0]), pl.ds(start, both.shape[1]))
    ref[at] = jnp.where(both, value.astype(BF16), ref[at])


def frame_rows(pieces):
    n, rows, width = pieces.shape
    return pieces.astype(F32).reshape(n * rows, width).astype(BF16)


def piece_rows(values, n):
    return values.reshape(n, values.shape[0] // n, values.shape[1]).astype(BF16)


def same_video(rows, frames):
    left = lax.broadcasted_iota(jnp.int32, (rows, 2 * rows), 0) // frames
    column = lax.broadcasted_iota(jnp.int32, (rows, 2 * rows), 1)
    right = jnp.where(column >= rows, column - rows, column) // frames
    return left == right


class Copies:
    def __init__(self, sems):
        self.sems, self.used = sems, 0

    def start(self, source, target):
        copy = pltpu.make_async_copy(source, target, self.sems.at[self.used])
        self.used += 1
        copy.start()
        return copy


def qkv_loads(copies, wqkv_ref, wqkv, width):
    parts = [pl.ds(part * width, width) for part in range(3)]
    return [copies.start(wqkv_ref.at[:, at], wqkv.at[:, at]) for at in parts]


def project_qkv(modded, wqkv, loads, packed, width):
    for part, load in enumerate(loads):
        load.wait()
        at = pl.ds(part * width, width)
        packed[:, at] = dot(modded, wqkv[:, at]).astype(BF16)


def split_kernel(n, video, x_ref, scatter_ref, *refs):
    out_ref = refs[-1]
    out_ref[...] = piece_rows(dot(scatter_ref[...], x_ref[video]), n)


def join_kernel(videos, *refs):
    gather_ref, out_ref = refs[videos], refs[-1]
    for video in range(videos):
        out_ref[video] = dot(gather_ref[...], frame_rows(refs[video][...])).astype(BF16)


def space_forward_kernel(
    n, block, video, with_cot, x_ref, cot_ref, mod_ref, wqkv_ref, wout_ref, scatter_ref, *refs
):
    sent_ref, packed_out, modded_out, attended_out, weights_out = refs[-14:-9]
    x, cot, modded, packed, attended, weights, wqkv, wout, sems = refs[-9:]
    width = x.shape[1]
    size = width // HEADS
    factor = size ** (-0.5)
    copies = Copies(sems)
    load_x = copies.start(x_ref.at[video], x)
    load_qkv = qkv_loads(copies, wqkv_ref, wqkv, width)
    load_out = copies.start(wout_ref, wout)
    if with_cot:
        load_cot = copies.start(cot_ref.at[video], cot)
    load_x.wait()
    normed, _ = norm_stats(x[...].astype(F32))
    modded[...] = (normed * (1.0 + mod_ref[video, 1:2, :]) + mod_ref[video, 0:1, :]).astype(BF16)
    stores = [copies.start(modded, modded_out)]
    project_qkv(modded[...], wqkv, load_qkv, packed, width)
    stores.append(copies.start(packed, packed_out))
    pairs = pair_windows(width)

    def one_block(g, carry):
        rows = pl.multiple_of(g * block, 16)
        for pair, (start, span, offset) in enumerate(pairs):
            first, both = pair_masks(block, span, offset, size)
            at = pl.ds(rows, block)
            query = packed[at, pl.ds(start, span)]
            key = packed[at, pl.ds(width + start, span)]
            value = packed[at, pl.ds(2 * width + start, span)]
            probs = probs_by_key(two_heads(query, first, both), key, factor, None).astype(BF16)
            weights[g * len(pairs) + pair] = probs
            put(attended, rows, start, both, per_query(probs, value, first))
        return carry

    lax.fori_loop(0, x.shape[0] // block, one_block, 0)
    stores.append(copies.start(attended, attended_out))
    stores.append(copies.start(weights, weights_out))
    load_out.wait()
    projected = dot(attended[...], wout[...])
    middle = (x[...].astype(F32) + mod_ref[video, 2:3, :] * projected).astype(BF16)
    pieces = piece_rows(dot(scatter_ref[...], middle), n)
    if with_cot:
        load_cot.wait()
        padded = pieces.shape[1]
        sent_ref[:, :padded, :] = pieces
        sent_ref[:, padded:, :] = piece_rows(dot(scatter_ref[...], cot[...]), n)
    else:
        sent_ref[...] = pieces
    for store in stores:
        store.wait()


def unit_stores(copies, core, width, left, right, outs):
    *sent_outs, right_out = outs
    other = (1 - core) * (2 * width)
    sources = [left.at[:, pl.ds(unit * width, width)] for unit in range(2)]
    sources += [
        right.at[:, pl.ds(pl.multiple_of(other + unit * width, 128), width)] for unit in range(2)
    ]
    return [copies.start(source, out) for source, out in zip(sources, sent_outs)] + [
        copies.start(right, right_out)
    ]


def time_kernel(
    n, block, frames, video, merged, joint, core_ref, middle_ref, cot_ref, mod_ref, wqkv_ref,
    wout_ref, gather_ref, scatter_ref, *refs
):
    n_out = 6 if joint else 7
    outs, scratch = refs[-10 - n_out : -10], refs[-10:]
    normed, x, up, left, packed, d_out, right, wqkv, wout, sems = scratch
    width = x.shape[1]
    size = width // HEADS
    factor = size ** (-0.5)
    copies = Copies(sems)
    load_qkv = qkv_loads(copies, wqkv_ref, wqkv, width)
    load_out = copies.start(wout_ref, wout)
    gather = gather_ref[...]
    if merged:
        padded = middle_ref.shape[1] // 2
        middle, cot = middle_ref[:, :padded, :], middle_ref[:, padded:, :]
    else:
        middle, cot = middle_ref[...], cot_ref[...]
    x[...] = dot(gather, frame_rows(middle)).astype(BF16)
    up[...] = dot(gather, frame_rows(cot)).astype(BF16)
    normed_now, inverse = norm_stats(x[...].astype(F32))
    normed[...] = normed_now
    left[:, 0:width] = (
        normed_now * (1.0 + mod_ref[video, 4:5, :]) + mod_ref[video, 3:4, :]
    ).astype(BF16)
    right[:, 3 * width :] = (mod_ref[video, 5:6, :] * up[...].astype(F32)).astype(BF16)
    project_qkv(left[:, 0:width], wqkv, load_qkv, packed, width)
    load_out.wait()
    d_out[...] = dot(right[:, 3 * width :], wout[...], NT).astype(BF16)
    keep = same_video(block, frames)

    def one_block(g, carry):
        rows = pl.multiple_of(g * block, 16)
        for start, span, offset in pair_windows(width):
            first, both = pair_masks(block, span, offset, size)
            at = pl.ds(rows, block)
            query = two_heads(packed[at, pl.ds(start, span)], first, both)
            key = packed[at, pl.ds(width + start, span)]
            value = packed[at, pl.ds(2 * width + start, span)]
            d_rows = two_heads(d_out[at, pl.ds(start, span)], first, both)
            probs = probs_by_key(query, key, factor, keep)
            weights = probs.astype(BF16)
            put(left, rows, width + start, both, per_query(weights, value, first))
            d_probs = dot(value, d_rows, NT)
            total = jnp.sum(probs * d_probs, 0, keepdims=True)
            d_scores = (probs * (d_probs - total) * factor).astype(BF16)
            put(right, rows, start, both, per_query(d_scores, key, first))
            put(right, rows, width + start, both, dot(d_scores, query))
            put(right, rows, 2 * width + start, both, dot(weights, d_rows))
        return carry

    lax.fori_loop(0, x.shape[0] // block, one_block, 0)
    stores = unit_stores(copies, core_ref[1] & 1, width, left, right, outs[-5:])
    d_modded = dot(right[:, 0 : 3 * width], wqkv[...], NT)
    d_middle = up[...].astype(F32) + norm_backward(
        d_modded, normed[...], inverse, mod_ref[video, 4:5, :]
    )
    d_pieces = piece_rows(dot(scatter_ref[...], d_middle.astype(BF16)), n)
    projected = dot(left[:, width:], wout[...])
    out = (x[...].astype(F32) + mod_ref[video, 5:6, :] * projected).astype(BF16)
    if joint:
        padded = d_pieces.shape[1]
        outs[0][:, :padded, :] = d_pieces
        outs[0][:, padded:, :] = piece_rows(dot(scatter_ref[...], out), n)
    else:
        outs[0][...] = d_pieces
        outs[1][0] = out
    for store in stores:
        store.wait()


def space_backward_kernel(
    block, video, core_ref, up_ref, mod_ref, wout_ref, gather_ref, packed_ref, modded_ref,
    attended_ref, weights_ref, *refs
):
    d_middle_ref, *unit_outs = refs[-12:-6]
    d_out, left, right, packed, wout, sems = refs[-6:]
    width = wout.shape[0]
    size = width // HEADS
    factor = size ** (-0.5)
    copies = Copies(sems)
    load_out = copies.start(wout_ref, wout)
    load_packed = copies.start(packed_ref, packed)
    loads = [
        copies.start(modded_ref, left.at[:, pl.ds(0, width)]),
        copies.start(attended_ref, left.at[:, pl.ds(width, width)]),
    ]
    padded = gather_ref.shape[1] // up_ref.shape[0]
    up = dot(gather_ref[...], frame_rows(up_ref[:, :padded, :]))
    d_middle_ref[...] = up.astype(BF16)
    right[:, 3 * width :] = (mod_ref[video, 2:3, :] * up).astype(BF16)
    load_out.wait()
    d_out[...] = dot(right[:, 3 * width :], wout[...], NT).astype(BF16)
    load_packed.wait()
    pairs = pair_windows(width)

    def one_block(g, carry):
        rows = pl.multiple_of(g * block, 16)
        for pair, (start, span, offset) in enumerate(pairs):
            first, both = pair_masks(block, span, offset, size)
            at = pl.ds(rows, block)
            query = two_heads(packed[at, pl.ds(start, span)], first, both)
            key = packed[at, pl.ds(width + start, span)]
            value = packed[at, pl.ds(2 * width + start, span)]
            d_rows = two_heads(d_out[at, pl.ds(start, span)], first, both)
            weights = weights_ref[g * len(pairs) + pair]
            probs = weights.astype(F32)
            d_probs = dot(value, d_rows, NT)
            total = jnp.sum(probs * d_probs, 0, keepdims=True) / jnp.sum(probs, 0, keepdims=True)
            d_scores = (probs * (d_probs - total) * factor).astype(BF16)
            put(right, rows, start, both, per_query(d_scores, key, first))
            put(right, rows, width + start, both, dot(d_scores, query))
            put(right, rows, 2 * width + start, both, dot(weights, d_rows))
        return carry

    lax.fori_loop(0, d_out.shape[0] // block, one_block, 0)
    for load in loads:
        load.wait()
    for store in unit_stores(copies, core_ref[1] & 1, width, left, right, unit_outs):
        store.wait()


def grad_input_kernel(video, right_ref, d_middle_ref, x_ref, mod_ref, wqkv_ref, *refs):
    out_ref, d_packed, sems = refs[-3:]
    width = out_ref.shape[1]
    Copies(sems).start(right_ref.at[:, pl.ds(0, 3 * width)], d_packed).wait()
    d_modded = dot(d_packed[...], wqkv_ref[...], NT)
    normed, inverse = norm_stats(x_ref[video].astype(F32))
    d_tokens = norm_backward(d_modded, normed, inverse, mod_ref[video, 1:2, :])
    out_ref[...] = (d_middle_ref[...].astype(F32) + d_tokens).astype(BF16)


def bit_of(place_ref, axis, bit):
    return (place_ref[0 if axis == "dp" else 1] >> bit) & 1


def emit_halves(rows, inner, mine, kept_ref, sent_ref):
    for outer in range(kept_ref.shape[0]):
        low = rows[2 * outer * inner : (2 * outer + 1) * inner, :]
        high = rows[(2 * outer + 1) * inner : (2 * outer + 2) * inner, :]
        kept_ref[outer] = jnp.where(mine == 0, low, high).astype(BF16)
        sent_ref[outer] = jnp.where(mine == 0, high, low).astype(BF16)


def weight_kernel(videos, cuts, steps, grad_scale, place_ref, *refs):
    right, units = refs[:videos], refs[videos : 9 * videos]
    sent = [units[4 * v : 4 * v + 4] for v in range(videos)]
    got = [units[4 * v : 4 * v + 4] for v in range(videos, 2 * videos)]
    outs = refs[-4 - 2 * len(cuts) : -4]
    left_rows, right_rows, total, sems = refs[-4:]
    width = left_rows.shape[1] // 2
    tokens = right[0].shape[0]
    copies = Copies(sems)
    core = place_ref[1] & 1
    own = pl.multiple_of(core * (2 * width), 128)
    waits = []
    for unit in range(2):
        now = []
        for video in range(videos):
            for place, (left, mine) in enumerate(((sent[video], right[video]), (got[video], None))):
                rows = pl.ds((2 * video + place) * tokens, tokens)
                at = pl.ds(unit * width, width)
                now.append(copies.start(left[unit], left_rows.at[rows, at]))
                source = (
                    left[2 + unit]
                    if mine is None
                    else mine.at[:, pl.ds(pl.multiple_of(own + unit * width, 128), width)]
                )
                now.append(copies.start(source, right_rows.at[rows, at]))
        waits.append(now)
    done = 0
    for part, ((low, high), (axis, bit, inner)) in enumerate(zip(cuts, steps)):
        for unit in range(2):
            start, stop = max(low, unit * width), min(high, (unit + 1) * width)
            if start >= stop:
                continue
            while done <= unit:
                for wait in waits[done]:
                    wait.wait()
                done += 1
            column = pl.multiple_of(core * width, 128) if unit else 0
            left = left_rows[:, pl.ds(column, width)]
            total[:, start - low : stop - low] = (
                dot(left, right_rows[:, start:stop], TN) * grad_scale
            )
        emit_halves(
            total, inner, bit_of(place_ref, axis, bit), outs[2 * part], outs[2 * part + 1]
        )


def stage_kernel(steps, place_ref, *refs):
    count = len(steps)
    total, outs = refs[-1], refs[-1 - 2 * count : -1]
    for part, (axis, bit, inner) in enumerate(steps):
        kept, got = refs[part], refs[count + part]
        each = kept.shape[1]
        for outer in range(kept.shape[0]):
            total[outer * each : (outer + 1) * each, :] = kept[outer].astype(F32) + got[
                outer
            ].astype(F32)
        emit_halves(
            total, inner, bit_of(place_ref, axis, bit), outs[2 * part], outs[2 * part + 1]
        )


def core_stage_kernel(count, place_ref, *refs):
    kept_out, sent_out = refs[-2:]
    rows, columns = refs[0].shape[1:]
    core = place_ref[1] & 1
    for part in range(count):
        total = refs[part][0].astype(F32) + refs[count + part][0].astype(F32)
        low, high = total[: rows // 2], total[rows // 2 :]
        at = slice(part * columns, (part + 1) * columns)
        kept_out[:, at] = jnp.where(core == 0, low, high).astype(BF16)
        sent_out[:, at] = jnp.where(core == 0, high, low).astype(BF16)


def assemble_kernel(place_ref, kept_ref, got_ref, qkv_ref, out_ref):
    width = out_ref.shape[1]
    core = place_ref[1] & 1
    kept, got = kept_ref[...].astype(F32), got_ref[...].astype(F32)
    low = jnp.where(core == 0, kept, got).astype(BF16)
    high = jnp.where(core == 0, got, kept).astype(BF16)
    qkv_ref[:, : 2 * width] = low
    qkv_ref[:, 2 * width :] = high[:, :width]
    out_ref[...] = high[:, width:]


def swap(x, axis, mask):
    size = lax.axis_size(axis)
    return lax.ppermute(x, axis, [(i, i ^ mask) for i in range(size)])


class Reduction:
    def __init__(self, place, width):
        dp_bits = [("dp", bit) for bit in range(lax.axis_size("dp").bit_length() - 1)]
        seq_bits = [("seq", bit) for bit in range(1, lax.axis_size("seq").bit_length() - 1)]
        self.place, self.width, self.columns = place, width, 2 * width // 3
        self.cuts = tuple((part * self.columns, (part + 1) * self.columns) for part in range(3))
        self.orders = (
            dp_bits + seq_bits,
            dp_bits[-1:] + seq_bits[:1] + dp_bits[:-1] + seq_bits[1:],
            seq_bits[:1] + dp_bits + seq_bits[1:],
        )
        self.bits = dp_bits[::-1] + seq_bits[::-1]
        self.step = 0

    def next_steps(self):
        least = self.width >> len(self.bits)
        steps, shapes = [], []
        for order in self.orders:
            left = [bit for bit in self.bits if bit not in order[: self.step]]
            above = left.index(order[self.step])
            inner = least << (len(left) - above - 1)
            steps.append((*order[self.step], inner))
            shapes += 2 * [shaped(1 << above, inner, self.columns)]
        return tuple(steps), tuple(shapes)

    def send(self, halves):
        self.kept = halves[0::2]
        self.got = [
            swap(half, order[self.step][0], 1 << order[self.step][1])
            for half, order in zip(halves[1::2], self.orders)
        ]
        self.step += 1

    def stage(self, deps=()):
        steps, shapes = self.next_steps()
        halves = call(
            "stage", 2, functools.partial(stage_kernel, steps), "s" + "v" * 6, shapes, "v" * 6,
            [pltpu.VMEM((self.width >> self.step, self.columns), F32)],
        )(self.place, *self.kept, *self.got, deps=deps)
        self.send(halves)
        return halves[0]

    def finish(self):
        while self.step < len(self.bits):
            self.stage()
        rows = self.width >> (len(self.bits) + 1)
        half = shaped(rows, 2 * self.width)
        kept, sent = call(
            "core_stage", 1, functools.partial(core_stage_kernel, 3), "s" + "v" * 6, (half, half),
            "vv",
        )(self.place, *self.kept, *self.got)
        return call(
            "assemble", 1, assemble_kernel, "svv",
            (shaped(rows, 3 * self.width), shaped(rows, self.width)), "vv",
        )(self.place, kept, swap(sent, "seq", 1))


def shards(frames_in, modulation, spatial_qkv, spatial_out, temporal_qkv, temporal_out, cotangent):
    n = lax.axis_size("seq")
    videos, frames, patches, width = frames_in.shape
    all_frames = frames * n
    tokens = frames * patches
    own_patches = patches // n
    rows = frames * own_patches
    padded = -(-rows // 8) * 8
    time_block = 6 * all_frames if own_patches % 6 == 0 else 3 * all_frames
    core = jnp.stack([lax.axis_index("dp"), lax.axis_index("seq")]).astype(jnp.int32)

    to_pieces = np.zeros((n * padded, tokens), np.float32)
    by_patch = np.zeros((tokens, n * padded), np.float32)
    for device in range(n):
        for f in range(frames):
            for p in range(own_patches):
                place = device * padded + f * own_patches + p
                to_pieces[place, f * patches + device * own_patches + p] = 1
                by_patch[p * all_frames + device * frames + f, place] = 1
    to_pieces, from_pieces = jnp.asarray(to_pieces, BF16), jnp.asarray(to_pieces.T, BF16)
    by_patch, from_patch = jnp.asarray(by_patch, BF16), jnp.asarray(by_patch.T, BF16)

    def exchange(pieces):
        return lax.all_to_all(pieces, "seq", split_axis=0, concat_axis=0, tiled=True)

    piece = shaped(n, padded, width)
    piece_pair = shaped(n, 2 * padded, width)
    row = shaped(tokens, width)
    three, four = shaped(tokens, 3 * width), shaped(tokens, 4 * width)
    all_rows = shaped(videos, tokens, width)
    weights_shape = (frames * (HEADS // 2), patches, 2 * patches)

    def vmem(*shape, dtype=BF16):
        return pltpu.VMEM(shape, dtype)

    def sems(count):
        return pltpu.SemaphoreType.DMA((count,))

    weight_refs = [vmem(width, 3 * width), vmem(width, width)]
    x = frames_in.reshape(videos, tokens, width)
    cot = cotangent.reshape(videos, tokens, width)

    def split(values, video, matrix, deps=()):
        return call("split", 3, functools.partial(split_kernel, n, video), "vv", piece, "v")(
            values, matrix, deps=deps
        )

    cot_first = split(cot, 0, to_pieces)
    deps = [cot_first]
    saved, arrived = [], []
    for v in range(videos):
        sent, *keep = call(
            "space_forward", 14,
            functools.partial(space_forward_kernel, n, patches, v, v > 0),
            "aavaav",
            (piece_pair if v > 0 else piece, three, row, row, shaped(*weights_shape)),
            "vaaaa",
            [
                vmem(tokens, width), vmem(tokens, width), vmem(tokens, width),
                vmem(tokens, 3 * width), vmem(tokens, width), vmem(*weights_shape),
                *weight_refs, sems(10),
            ],
        )(x, cot, modulation, spatial_qkv, spatial_out, to_pieces, deps=deps)
        if v == 0:
            cot_pieces = exchange(cot_first)
            deps = [cot_pieces]
        else:
            deps = [sent]
        arrived.append(exchange(sent))
        saved.append(keep)

    def exchange_units(sent):
        return [swap(unit, "seq", 1) for unit in sent]

    returned, time_units = [], []
    last = videos - 1
    for v in range(videos):
        joint = v != last
        outs = call(
            "time", 25,
            functools.partial(time_kernel, n, time_block, all_frames, v, v > 0, joint),
            "svvvaavv",
            ((piece_pair,) if joint else (piece, shaped(1, tokens, width))) + 4 * (row,) + (four,),
            ("v" if joint else "vv") + "aaaaa",
            [
                vmem(tokens, width, dtype=F32), vmem(tokens, width), vmem(tokens, width),
                vmem(tokens, 2 * width), vmem(tokens, 3 * width), vmem(tokens, width),
                vmem(tokens, 4 * width), *weight_refs, sems(9),
            ],
        )(
            core, arrived[v], cot_pieces if v == 0 else core, modulation, temporal_qkv,
            temporal_out, by_patch, from_patch, deps=deps,
        )
        deps = [outs[-1]]
        returned.append(exchange(outs[0]))
        time_units.append((list(outs[-5:-1]), outs[-1], exchange_units(outs[-5:-1])))
    last_out = outs[1]

    grad_scale = (videos * lax.axis_size("dp") * all_frames * patches) ** (-0.5)

    def weights(units, deps=()):
        reduction = Reduction(core, width)
        steps, shapes = reduction.next_steps()
        sent, right, got = zip(*units)
        halves = call(
            "weights", 10,
            functools.partial(weight_kernel, videos, reduction.cuts, steps, grad_scale),
            "s" + "a" * (9 * videos), shapes, "v" * 6,
            [
                vmem(2 * videos * tokens, 2 * width), vmem(2 * videos * tokens, 2 * width),
                vmem(width, reduction.columns, dtype=F32), sems(8 * videos),
            ],
        )(core, *right, *sum(sent, []), *sum(got, []), deps=deps)
        reduction.send(halves)
        return reduction, halves[0]

    def grad_of(video, units, d_middle, deps=()):
        return call(
            "grad_input", 8, functools.partial(grad_input_kernel, video), "avvvv", row, "v",
            [vmem(tokens, 3 * width), sems(1)],
        )(units[1], d_middle, x, modulation, spatial_qkv, deps=deps)

    d_middles, space_units, grad_input = [], [], []
    for v in range(videos):
        d_middle, *sent, right = call(
            "space_backward", 15, functools.partial(space_backward_kernel, patches, v),
            "svvavaaav",
            (row,) + 4 * (row,) + (four,),
            "vaaaaa",
            [
                vmem(tokens, width), vmem(tokens, 2 * width), vmem(tokens, 4 * width),
                vmem(tokens, 3 * width), vmem(width, width), sems(9),
            ],
        )(
            core, returned[v], modulation, spatial_out, from_pieces, *saved[v], deps=deps
        )
        if v == 0:
            last_pieces = split(last_out, 0, from_patch, deps=[right])
            time_sum, began = weights(time_units, deps=[last_pieces])
            deps = [began]
            last_back = exchange(last_pieces)
        d_middles.append(d_middle)
        space_units.append((sent, right, exchange_units(sent)))
    began = time_sum.stage(deps=[right])
    space_sum, began = weights(space_units, deps=[began, last_back])
    began = time_sum.stage(deps=[began])
    for v in range(videos):
        grad_input.append(grad_of(v, space_units[v], d_middles[v], deps=[began]))
        began = grad_input[-1]
    began = space_sum.stage(deps=[began])
    out_pieces = [r[:, padded:, :] for r in returned[:-1]] + [last_back]
    block_out = call(
        "join", 4, functools.partial(join_kernel, videos), "v" * (videos + 1), all_rows, "v"
    )(*out_pieces, from_pieces, deps=[began])
    grad_input = jnp.stack(grad_input)
    grad_time, grad_space = time_sum.finish(), space_sum.finish()
    return (
        block_out.reshape(frames_in.shape), grad_input.reshape(frames_in.shape),
        *grad_space, *grad_time,
    )


def solution(mesh):
    return jax.shard_map(
        shards,
        mesh=mesh,
        in_specs=(
            P("dp", "seq", None, None),
            P("dp", None, None),
            P(),
            P(),
            P(),
            P(),
            P("dp", "seq", None, None),
        ),
        out_specs=(
            P("dp", "seq", None, None),
            P("dp", "seq", None, None),
            P(("dp", "seq"), None),
            P(("dp", "seq"), None),
            P(("dp", "seq"), None),
            P(("dp", "seq"), None),
        ),
        check_vma=False,
    )
```

time: 1010 us -> 333 us (0.33)
  waiting for transfers between devices: 548 us -> 78.6 us
  matrix products: 193 us -> 0 us
  local copies, waits for them, and re-layouts: 204 us -> 14.1 us
  Pallas kernels: 0 us -> 173 us
  starting transfers between devices: 20 us -> 58.6 us
  other arithmetic: 23.4 us -> 1.78 us
  between operations: 14.6 us -> 1.35 us
    unnamed x10 -> x0, waiting for transfers between devices: 471 us -> none
    dot_general x23 -> x0, matrix products: 184 us -> none  [the longest x4 31.6 us: weight_term(): jnp.einsum('vfpd,vfpc->dc', left_rows, right_rows, preferred_element_type...]
    pallas_call x0 -> x23, Pallas kernels: none -> 173 us  [run(): pl.pallas_call(body, out_shape=out_shape, in_specs=[pl.BlockSpec(memory_s...]
    reshape x25 -> x0, local copies, waits for them, and re-layouts: 145 us -> none  [the longest x8 62.7 us: reduce_terms(): piece.reshape(data_count, seq_count, piece.shape[0] // (data_count * seq_...]
    ppermute x0 -> x42, waiting for transfers between devices: none -> 49 us  [swap(): return lax.ppermute(x, axis, [(i, i ^ mask) for i in range(size)])]
    all_to_all x4 -> x6, waiting for transfers between devices: 77 us -> 29.6 us  [exchange(): lax.all_to_all(pieces, 'seq', split_axis=0, concat_axis=0, tiled=True)]
    ppermute x0 -> x42, starting transfers between devices: none -> 31.6 us  [swap(): return lax.ppermute(x, axis, [(i, i ^ mask) for i in range(size)])]
    convert_element_type x10 -> x0, local copies, waits for them, and re-layouts: 24.7 us -> none  [the longest x2 6.95 us: branch_forward(): attended = mixed_heads.reshape(tokens_in.shape).astype(jnp.bfloat16)]
  transfers between devices with their start and end apart: 9 -> 48, of which waited for: 6 -> 12; matrix products, arithmetic and copies ran while one was open for 9% -> 1% of each run, Pallas kernels for 0% -> 52%
where the time goes in v1:
time: 333 us; the launch traced here: 327 us
  Pallas kernels  173 us (52%)
  waiting for transfers between devices  78.6 us (24%)
  starting transfers between devices  58.6 us (18%)
  local copies, waits for them, and re-layouts  14.1 us (4%)
    pallas_call x23, Pallas kernels, run(): pl.pallas_call(body, out_shape=out_shape, in_specs=[pl.BlockSpec(memory_s...  173 us
    ppermute x42, waiting for transfers between devices, swap(): return lax.ppermute(x, axis, [(i, i ^ mask) for i in range(size)])  49 us
    ppermute x42, starting transfers between devices, swap(): return lax.ppermute(x, axis, [(i, i ^ mask) for i in range(size)])  31.6 us
    all_to_all x6, waiting for transfers between devices, exchange(): lax.all_to_all(pieces, 'seq', split_axis=0, concat_axis=0, tiled=True)  29.6 us
    all_to_all x6, starting transfers between devices, exchange(): lax.all_to_all(pieces, 'seq', split_axis=0, concat_axis=0, tiled=True)  26.9 us
    unnamed x79, local copies, waits for them, and re-layouts  14 us
  transfers between devices with their start and end apart: 48, of which 12 were waited for; matrix products, arithmetic and copies ran while one was open for 1% of the time, Pallas kernels for 52%

profile of v1, /device:TPU:0, one launch (start us, length us, event | category | flops | bytes accessed | tf_op | source)
XLA Modules:
  0.0 327.0 jit_solution(10547714324758294152)
XLA Ops:
  2.9 1.4 split.2.refs_0_
  4.3 6.3 %all-to-all-start.1 = ((bf16[8,40,1152]{2,1,0:T(8,128)(2,1)}), bf16[8,40,1152]{2,1,0:T(8,128)(2,1)S(1)}, u32[]{:S(2)}, u32[]{:S(2)}) async-start(bf16[8,40,1152]{2,1,0:T(8,128)(2,1)} %split.2.refs_0_), calls=%async_computation.1 | async-start | bytes 1474560 | tf_op jit(solution)/shard_map/all_to_all | solution.py:545
  11.3 14.2 %space_forward.2 = (bf16[8,40,1152]{2,1,0:T(8,128)(2,1)}, bf16[288,3456]{1,0:T(8,128)(2,1)}, bf16[288,1152]{1,0:T(8,128)(2,1)}, bf16[288,1152]{1,0:T(8,128)(2,1)}, bf16[16,144,288]{2,1,0:T(8,128)(2,1)}) custom-call(bf16[2,288,1152]{2,1,0:T(8,128)(2,1)} %bitcast.12, bf16[2,288,1152]{2,1,0:T(8,128)(2,1)} %bitcast.8, f32[2,6,1152]{2,1,0:T(8,128)} %copy.17.mod_ref, ...), custom_call_target="tpu_custom_call" | custom-call | flops 14000000000 | bytes 14000000 | tf_op jit(solution)/shard_map/space_forward/pallas_call | solution.py:33
  25.5 5.0 %all-to-all-done.1.refs_0_.cot_ref = bf16[8,40,1152]{2,1,0:T(8,128)(2,1)S(1)} async-done(((bf16[8,40,1152]{2,1,0:T(8,128)(2,1)}), bf16[8,40,1152]{2,1,0:T(8,128)(2,1)S(1)}, u32[]{:S(2)}, u32[]{:S(2)}) %all-to-all-start.1) | async-done | bytes 737312 | tf_op jit(solution)/shard_map/all_to_all | solution.py:545
  30.6 3.7 %all-to-all-start = ((bf16[8,40,1152]{2,1,0:T(8,128)(2,1)}), bf16[8,40,1152]{2,1,0:T(8,128)(2,1)S(1)}, u32[]{:S(2)}, u32[]{:S(2)}) async-start(bf16[8,40,1152]{2,1,0:T(8,128)(2,1)} %get-tuple-element.97), calls=%async_computation | async-start | bytes 1474560 | tf_op jit(solution)/shard_map/all_to_all | solution.py:545
  34.3 15.2 %space_forward.3 = (bf16[8,80,1152]{2,1,0:T(8,128)(2,1)}, bf16[288,3456]{1,0:T(8,128)(2,1)}, bf16[288,1152]{1,0:T(8,128)(2,1)}, bf16[288,1152]{1,0:T(8,128)(2,1)}, bf16[16,144,288]{2,1,0:T(8,128)(2,1)}) custom-call(bf16[2,288,1152]{2,1,0:T(8,128)(2,1)} %bitcast.13, bf16[2,288,1152]{2,1,0:T(8,128)(2,1)} %bitcast.9, f32[2,6,1152]{2,1,0:T(8,128)} %copy.17.mod_ref, ...), custom_call_target="tpu_custom_call" | custom-call | flops 14000000000 | bytes 14000000 | tf_op jit(solution)/shard_map/space_forward/pallas_call | solution.py:33
  49.5 4.7 %all-to-all-done.middle_ref = bf16[8,40,1152]{2,1,0:T(8,128)(2,1)S(1)} async-done(((bf16[8,40,1152]{2,1,0:T(8,128)(2,1)}), bf16[8,40,1152]{2,1,0:T(8,128)(2,1)S(1)}, u32[]{:S(2)}, u32[]{:S(2)}) %all-to-all-start) | async-done | bytes 737312 | tf_op jit(solution)/shard_map/all_to_all | solution.py:545
  54.1 3.8 %all-to-all-start.3 = ((bf16[8,80,1152]{2,1,0:T(8,128)(2,1)}), bf16[8,80,1152]{2,1,0:T(8,128)(2,1)S(1)}, u32[]{:S(2)}, u32[]{:S(2)}) async-start(bf16[8,80,1152]{2,1,0:T(8,128)(2,1)} %get-tuple-element.98.refs_0_), calls=%async_computation.3 | async-start | bytes 2949120 | tf_op jit(solution)/shard_map/all_to_all | solution.py:545
  58.5 24.8 %time.2 = (bf16[8,80,1152]{2,1,0:T(8,128)(2,1)}, bf16[288,1152]{1,0:T(8,128)(2,1)}, bf16[288,1152]{1,0:T(8,128)(2,1)}, bf16[288,1152]{1,0:T(8,128)(2,1)}, bf16[2...) custom-call(s32[2]{0:T(128)} %pad_add_fusion.core_ref.cot_ref.place_ref, bf16[8,40,1152]{2,1,0:T(8,128)(2,1)} %copy-done.28, ...), custom_call_target="tpu_custom_call" | custom-call | flops 24999999488 | bytes 25000000 | tf_op jit(solution)/shard_map/time/pallas_call | solution.py:33
  83.3 10.2 %all-to-all-done.3.middle_ref = bf16[8,80,1152]{2,1,0:T(8,128)(2,1)S(1)} async-done(((bf16[8,80,1152]{2,1,0:T(8,128)(2,1)}), bf16[8,80,1152]{2,1,0:T(8,128)(2,1)S(1)}, u32[]{:S(2)}, u32[]{:S(2)}) %all-to-all-start.3) | async-done | bytes 1474592 | tf_op jit(solution)/shard_map/all_to_all | solution.py:545
  93.6 4.0 %all-to-all-start.2 = ((bf16[8,80,1152]{2,1,0:T(8,128)(2,1)}), bf16[8,80,1152]{2,1,0:T(8,128)(2,1)S(1)}, u32[]{:S(2)}, u32[]{:S(2)}) async-start(bf16[8,80,1152]{2,1,0:T(8,128)(2,1)} %get-tuple-element.99), calls=%async_computation.2 | async-start | bytes 2949120 | tf_op jit(solution)/shard_map/all_to_all | solution.py:545
  98.7 24.4 %time.3 = (bf16[8,40,1152]{2,1,0:T(8,128)(2,1)}, bf16[1,288,1152]{2,1,0:T(8,128)(2,1)}, bf16[288,1152]{1,0:T(8,128)(2,1)}, bf16[288,1152]{1,0:T(8,128)(2,1)}, bf...) custom-call(s32[2]{0:T(128)} %pad_add_fusion.core_ref.cot_ref.place_ref, ...), custom_call_target="tpu_custom_call" | custom-call | flops 24999999488 | bytes 25000000 | tf_op jit(solution)/shard_map/time/pallas_call | solution.py:33
  123.6 9.6 %all-to-all-done.2.up_ref = bf16[8,80,1152]{2,1,0:T(8,128)(2,1)S(1)} async-done(((bf16[8,80,1152]{2,1,0:T(8,128)(2,1)}), bf16[8,80,1152]{2,1,0:T(8,128)(2,1)S(1)}, u32[]{:S(2)}, u32[]{:S(2)}) %all-to-all-start.2) | async-done | bytes 1474592 | tf_op jit(solution)/shard_map/all_to_all | solution.py:545
  133.2 3.7 %all-to-all-start.5 = ((bf16[8,40,1152]{2,1,0:T(8,128)(2,1)}), bf16[8,40,1152]{2,1,0:T(8,128)(2,1)S(1)}, u32[]{:S(2)}, u32[]{:S(2)}) async-start(bf16[8,40,1152]{2,1,0:T(8,128)(2,1)} %get-tuple-element.108), calls=%async_computation.5 | async-start | bytes 1474560 | tf_op jit(solution)/shard_map/all_to_all | solution.py:545
  138.0 14.4 %space_backward.2 = (bf16[288,1152]{1,0:T(8,128)(2,1)}, bf16[288,1152]{1,0:T(8,128)(2,1)}, bf16[288,1152]{1,0:T(8,128)(2,1)}, bf16[288,1152]{1,0:T(8,128)(2,1)},...) custom-call(s32[2]{0:T(128)} %pad_add_fusion.core_ref.cot_ref.place_ref, bf16[8,80,1152]{2,1,0:T(8,128)(2,1)} %copy-done.23, ...), custom_call_target="tpu_custom_call" | custom-call | flops 15000000512 | bytes 15000000 | tf_op jit(solution)/shard_map/space_backward/pallas_call | solution.py:33
  152.4 1.7 copy-done.19
  154.1 1.4 split.3.refs_18_
  158.0 15.1 %weights.2 = (bf16[2,288,768]{2,1,0:T(8,128)(2,1)}, bf16[2,288,768]{2,1,0:T(8,128)(2,1)}, bf16[1,576,768]{2,1,0:T(8,128)(2,1)}, bf16[1,576,768]{2,1,0:T(8,128)(2...) custom-call(s32[2]{0:T(128)} %pad_add_fusion.core_ref.cot_ref.place_ref, ...), custom_call_target="tpu_custom_call" | custom-call | flops 10000000000 | bytes 10000000 | tf_op jit(solution)/shard_map/weights/pallas_call | solution.py:33
  173.1 1.5 collective-permute-start.16
  174.6 1.5 collective-permute-start.17
  176.2 5.4 %all-to-all-start.4 = ((bf16[8,40,1152]{2,1,0:T(8,128)(2,1)}), bf16[8,40,1152]{2,1,0:T(8,128)(2,1)S(1)}, u32[]{:S(2)}, u32[]{:S(2)}) async-start(bf16[8,40,1152]{2,1,0:T(8,128)(2,1)} %split.3.refs_18_), calls=%async_computation.4 | async-start | bytes 1474560 | tf_op jit(solution)/shard_map/all_to_all | solution.py:545
  181.5 2.1 collective-permute-start.18
  183.7 14.2 %space_backward.3 = (bf16[288,1152]{1,0:T(8,128)(2,1)}, bf16[288,1152]{1,0:T(8,128)(2,1)}, bf16[288,1152]{1,0:T(8,128)(2,1)}, bf16[288,1152]{1,0:T(8,128)(2,1)},...) custom-call(s32[2]{0:T(128)} %pad_add_fusion.core_ref.cot_ref.place_ref, bf16[8,40,1152]{2,1,0:T(8,128)(2,1)} %copy-done.26, ...), custom_call_target="tpu_custom_call" | custom-call | flops 15000000512 | bytes 15000000 | tf_op jit(solution)/shard_map/space_backward/pallas_call | solution.py:33
  199.0 16.6 %collective-permute-done.18.refs_5_ = bf16[8,72,768]{2,1,0:T(8,128)(2,1)S(1)} collective-permute-done((bf16[8,72,768]{2,1,0:T(8,128)(2,1)}, bf16[8,72,768]{2,1,0:T(8,128)(2,1)S(1)}, u32[]{:S(2)}, u32[]{:S(2)}) %collective-permute-start.18) | collective-permute-done | bytes 884768 | tf_op jit(solution)/shard_map/ppermute | solution.py:462
  215.6 1.7 copy-done
  217.3 2.0 stage.6
  223.2 15.2 %weights.3 = (bf16[2,288,768]{2,1,0:T(8,128)(2,1)}, bf16[2,288,768]{2,1,0:T(8,128)(2,1)}, bf16[1,576,768]{2,1,0:T(8,128)(2,1)}, bf16[1,576,768]{2,1,0:T(8,128)(2...) custom-call(s32[2]{0:T(128)} %pad_add_fusion.core_ref.cot_ref.place_ref, ...), custom_call_target="tpu_custom_call" | custom-call | flops 10000000000 | bytes 10000000 | tf_op jit(solution)/shard_map/weights/pallas_call | solution.py:33
  238.5 1.6 collective-permute-start.19
  240.0 1.5 collective-permute-start.20
  241.6 1.6 collective-permute-start.21
  246.4 9.8 %grad_input.2.refs_0_ = bf16[288,1152]{1,0:T(8,128)(2,1)} custom-call(bf16[288,4608]{1,0:T(8,128)(2,1)} %get-tuple-element.107.refs_0_.right_ref, bf16[288,1152]{1,0:T(8,128)(2,1)} %get-tuple-element.144.d_middle_ref, bf16[2,288,1152]{2,1,0:T(8,128)(2,1)} %bitcast.14, f32[2,6,1152]{2,1,0:T(8,128)} %copy.17.mod_ref, bf16[1152,3456]{1,0:T(8,128)(2,1)} %wqkv_ref.11, ...), custom_call_target="tpu_custom_call" | custom-call | flops 8000000000 | bytes 8000000 | tf_op jit(solution)/shard_map/grad_input/pallas_call | solution.py:33
  256.2 9.7 %grad_input.3.refs_6_ = bf16[288,1152]{1,0:T(8,128)(2,1)} custom-call(bf16[288,4608]{1,0:T(8,128)(2,1)} %get-tuple-element.122.refs_6_.refs_1_.right_ref, bf16[288,1152]{1,0:T(8,128)(2,1)} %get-tuple-element.143.d_middle_ref, bf16[2,288,1152]{2,1,0:T(8,128)(2,1)} %bitcast.15, f32[2,6,1152]{2,1,0:T(8,128)} %copy.17.mod_ref, bf16[1152,3456]{1,0:T(8,128)(2,1)} %wqkv_ref.11, ...), custom_call_target="tpu_custom_call" | custom-call | flops 8000000000 | bytes 8000000 | tf_op jit(solution)/shard_map/grad_input/pallas_call | solution.py:33
  267.1 1.4 stage.8
  269.0 1.6 collective-permute-start.26
  271.2 1.5 collective-permute-start.36
  272.7 1.5 collective-permute-start.37
  274.2 11.3 %collective-permute-done.36.refs_4_ = bf16[1,144,768]{2,1,0:T(8,128)(2,1)S(1)} collective-permute-done((bf16[1,144,768]{2,1,0:T(8,128)(2,1)S(1)}, bf16[1,144,768]{2,1,0:T(8,128)(2,1)S(1)}, u32[]{:S(2)}, u32[]{:S(2)}) %collective-permute-start.36) | collective-permute-done | bytes 221216 | tf_op jit(solution)/shard_map/ppermute | solution.py:462
  286.3 2.5 collective-permute-start.38
  291.0 1.5 collective-permute-start.30
  293.0 1.8 collective-permute-done.38.refs_3_
  295.9 4.4 %collective-permute-done.39.refs_4_ = bf16[1,72,768]{2,1,0:T(8,128)(2,1)S(1)} collective-permute-done((bf16[1,72,768]{2,1,0:T(8,128)(2,1)S(1)}, bf16[1,72,768]{2,1,0:T(8,128)(2,1)S(1)}, u32[]{:S(2)}, u32[]{:S(2)}) %collective-permute-start.39) | collective-permute-done | bytes 110624 | tf_op jit(solution)/shard_map/ppermute | solution.py:462
  300.3 2.4 collective-permute-done.40.refs_5_
  304.3 2.9 collective-permute-start.32
  308.5 1.3 assemble.3
  309.9 7.7 %collective-permute-done.31.refs_3_ = bf16[1,72,768]{2,1,0:T(8,128)(2,1)S(1)} collective-permute-done((bf16[1,72,768]{2,1,0:T(8,128)(2,1)S(1)}, bf16[1,72,768]{2,1,0:T(8,128)(2,1)S(1)}, u32[]{:S(2)}, u32[]{:S(2)}) %collective-permute-start.31) | collective-permute-done | bytes 110624 | tf_op jit(solution)/shard_map/ppermute | solution.py:462
  317.6 2.4 collective-permute-done.32.refs_4_
  320.0 2.3 collective-permute-done.33.refs_5_
  323.5 2.0 join.1
  (153 shorter events, 28.9 us)
Async XLA Ops:
  4.3 26.3 %all-to-all-start.1 = ((bf16[8,40,1152]{2,1,0:T(8,128)(2,1)}), bf16[8,40,1152]{2,1,0:T(8,128)(2,1)S(1)}, u32[]{:S(2)}, u32[]{:S(2)}) async-start(bf16[8,40,1152]{2,1,0:T(8,128)(2,1)} %split.2.refs_0_), calls=%async_computation.1 | async-start | bytes 1474560 | tf_op jit(solution)/shard_map/all_to_all | solution.py:545
  30.6 23.6 %all-to-all-start = ((bf16[8,40,1152]{2,1,0:T(8,128)(2,1)}), bf16[8,40,1152]{2,1,0:T(8,128)(2,1)S(1)}, u32[]{:S(2)}, u32[]{:S(2)}) async-start(bf16[8,40,1152]{2,1,0:T(8,128)(2,1)} %get-tuple-element.97), calls=%async_computation | async-start | bytes 1474560 | tf_op jit(solution)/shard_map/all_to_all | solution.py:545
  54.1 39.4 %all-to-all-start.3 = ((bf16[8,80,1152]{2,1,0:T(8,128)(2,1)}), bf16[8,80,1152]{2,1,0:T(8,128)(2,1)S(1)}, u32[]{:S(2)}, u32[]{:S(2)}) async-start(bf16[8,80,1152]{2,1,0:T(8,128)(2,1)} %get-tuple-element.98.refs_0_), calls=%async_computation.3 | async-start | bytes 2949120 | tf_op jit(solution)/shard_map/all_to_all | solution.py:545
  93.6 39.6 %all-to-all-start.2 = ((bf16[8,80,1152]{2,1,0:T(8,128)(2,1)}), bf16[8,80,1152]{2,1,0:T(8,128)(2,1)S(1)}, u32[]{:S(2)}, u32[]{:S(2)}) async-start(bf16[8,80,1152]{2,1,0:T(8,128)(2,1)} %get-tuple-element.99), calls=%async_computation.2 | async-start | bytes 2949120 | tf_op jit(solution)/shard_map/all_to_all | solution.py:545
  97.6 39.4 %collective-permute-start = (bf16[288,1152]{1,0:T(8,128)(2,1)}, bf16[288,1152]{1,0:T(8,128)(2,1)}, u32[]{:S(2)}, u32[]{:S(2)}) collective-permute-start(bf16[288,1152]{1,0:T(8,128)(2,1)} %get-tuple-element.113.refs_2_), channel_id=1, source_target_pairs={{0,1},{1,0},{2,3},{3,2},{4,5},{5,4},{6,7},{7,6},{8,9},{9,8},{10,11... | collective-permute-start | bytes 1990664 | tf_op jit(solution)/shard_map/ppermute | solution.py:462
  98.1 39.4 %collective-permute-start.1 = (bf16[288,1152]{1,0:T(8,128)(2,1)}, bf16[288,1152]{1,0:T(8,128)(2,1)}, u32[]{:S(2)}, u32[]{:S(2)}) collective-permute-start(bf16[288,1152]{1,0:T(8,128)(2,1)} %get-tuple-element.114.refs_3_), channel_id=1, source_target_pairs={{0,1},{1,0},{2,3},{3,2},{4,5},{5,4},{6,7},{7,6},{8,9},{9,8},{10,11... | collective-permute-start | bytes 1990664 | tf_op jit(solution)/shard_map/ppermute | solution.py:462
  98.1 39.4 %collective-permute-start.2 = (bf16[288,1152]{1,0:T(8,128)(2,1)}, bf16[288,1152]{1,0:T(8,128)(2,1)}, u32[]{:S(2)}, u32[]{:S(2)}) collective-permute-start(bf16[288,1152]{1,0:T(8,128)(2,1)} %get-tuple-element.115.refs_4_), channel_id=1, source_target_pairs={{0,1},{1,0},{2,3},{3,2},{4,5},{5,4},{6,7},{7,6},{8,9},{9,8},{10,11... | collective-permute-start | bytes 1990664 | tf_op jit(solution)/shard_map/ppermute | solution.py:462
  98.6 57.0 %collective-permute-start.3 = (bf16[288,1152]{1,0:T(8,128)(2,1)}, bf16[288,1152]{1,0:T(8,128)(2,1)}, u32[]{:S(2)}, u32[]{:S(2)}) collective-permute-start(bf16[288,1152]{1,0:T(8,128)(2,1)} %get-tuple-element.116.refs_5_), channel_id=1, source_target_pairs={{0,1},{1,0},{2,3},{3,2},{4,5},{5,4},{6,7},{7,6},{8,9},{9,8},{10,11... | collective-permute-start | bytes 1990664 | tf_op jit(solution)/shard_map/ppermute | solution.py:462
  123.0 32.6 %collective-permute-start.4 = (bf16[288,1152]{1,0:T(8,128)(2,1)}, bf16[288,1152]{1,0:T(8,128)(2,1)S(1)}, u32[]{:S(2)}, u32[]{:S(2)}) collective-permute-start(bf16[288,1152]{1,0:T(8,128)(2,1)} %get-tuple-element.117.refs_6_), channel_id=1, source_target_pairs={{0,1},{1,0},{2,3},{3,2},{4,5},{5,4},{6,7},{7,6},{8,9},{9,8},{10,11... | collective-permute-start | bytes 1990664 | tf_op jit(solution)/shard_map/ppermute | solution.py:462
  133.2 43.0 %all-to-all-start.5 = ((bf16[8,40,1152]{2,1,0:T(8,128)(2,1)}), bf16[8,40,1152]{2,1,0:T(8,128)(2,1)S(1)}, u32[]{:S(2)}, u32[]{:S(2)}) async-start(bf16[8,40,1152]{2,1,0:T(8,128)(2,1)} %get-tuple-element.108), calls=%async_computation.5 | async-start | bytes 1474560 | tf_op jit(solution)/shard_map/all_to_all | solution.py:545
  136.9 19.1 %collective-permute-start.5 = (bf16[288,1152]{1,0:T(8,128)(2,1)}, bf16[288,1152]{1,0:T(8,128)(2,1)S(1)}, u32[]{:S(2)}, u32[]{:S(2)}) collective-permute-start(bf16[288,1152]{1,0:T(8,128)(2,1)} %get-tuple-element.118.refs_7_), channel_id=1, source_target_pairs={{0,1},{1,0},{2,3},{3,2},{4,5},{5,4},{6,7},{7,6},{8,9},{9,8},{10,11... | collective-permute-start | bytes 1990664 | tf_op jit(solution)/shard_map/ppermute | solution.py:462
  137.4 18.7 %collective-permute-start.6 = (bf16[288,1152]{1,0:T(8,128)(2,1)}, bf16[288,1152]{1,0:T(8,128)(2,1)S(1)}, u32[]{:S(2)}, u32[]{:S(2)}) collective-permute-start(bf16[288,1152]{1,0:T(8,128)(2,1)} %get-tuple-element.119.refs_8_), channel_id=1, source_target_pairs={{0,1},{1,0},{2,3},{3,2},{4,5},{5,4},{6,7},{7,6},{8,9},{9,8},{10,11... | collective-permute-start | bytes 1990664 | tf_op jit(solution)/shard_map/ppermute | solution.py:462
  137.5 18.6 %collective-permute-start.7 = (bf16[288,1152]{1,0:T(8,128)(2,1)}, bf16[288,1152]{1,0:T(8,128)(2,1)S(1)}, u32[]{:S(2)}, u32[]{:S(2)}) collective-permute-start(bf16[288,1152]{1,0:T(8,128)(2,1)} %get-tuple-element.120.refs_9_), channel_id=1, source_target_pairs={{0,1},{1,0},{2,3},{3,2},{4,5},{5,4},{6,7},{7,6},{8,9},{9,8},{10,11... | collective-permute-start | bytes 1990664 | tf_op jit(solution)/shard_map/ppermute | solution.py:462
  155.5 26.0 %collective-permute-start.8 = (bf16[288,1152]{1,0:T(8,128)(2,1)}, bf16[288,1152]{1,0:T(8,128)(2,1)}, u32[]{:S(2)}, u32[]{:S(2)}) collective-permute-start(bf16[288,1152]{1,0:T(8,128)(2,1)} %get-tuple-element.123.refs_2_), channel_id=1, source_target_pairs={{0,1},{1,0},{2,3},{3,2},{4,5},{5,4},{6,7},{7,6},{8,9},{9,8},{10,11... | collective-permute-start | bytes 1990664 | tf_op jit(solution)/shard_map/ppermute | solution.py:462
  155.6 42.2 %collective-permute-start.9 = (bf16[288,1152]{1,0:T(8,128)(2,1)}, bf16[288,1152]{1,0:T(8,128)(2,1)}, u32[]{:S(2)}, u32[]{:S(2)}) collective-permute-start(bf16[288,1152]{1,0:T(8,128)(2,1)} %get-tuple-element.124.refs_3_), channel_id=1, source_target_pairs={{0,1},{1,0},{2,3},{3,2},{4,5},{5,4},{6,7},{7,6},{8,9},{9,8},{10,11... | collective-permute-start | bytes 1990664 | tf_op jit(solution)/shard_map/ppermute | solution.py:462
  156.1 41.9 %collective-permute-start.10 = (bf16[288,1152]{1,0:T(8,128)(2,1)}, bf16[288,1152]{1,0:T(8,128)(2,1)}, u32[]{:S(2)}, u32[]{:S(2)}) collective-permute-start(bf16[288,1152]{1,0:T(8,128)(2,1)} %get-tuple-element.125.refs_4_), channel_id=1, source_target_pairs={{0,1},{1,0},{2,3},{3,2},{4,5},{5,4},{6,7},{7,6},{8,9},{9,8},{10,11... | collective-permute-start | bytes 1990664 | tf_op jit(solution)/shard_map/ppermute | solution.py:462
  173.1 25.3 %collective-permute-start.16 = (bf16[2,288,768]{2,1,0:T(8,128)(2,1)}, bf16[2,288,768]{2,1,0:T(8,128)(2,1)S(1)}, u32[]{:S(2)}, u32[]{:S(2)}) collective-permute-start(bf16[2,288,768]{2,1,0:T(8,128)(2,1)} %get-tuple-element.133), channel_id=1, source_target_pairs={{0,8},{8,0},{16,24},{24,16},{1,9},{9,1},{17,25},{25,17},{2,10},{10... | collective-permute-start | bytes 2654216 | tf_op jit(solution)/shard_map/ppermute | solution.py:462
  174.6 23.9 %collective-permute-start.17 = (bf16[1,576,768]{2,1,0:T(8,128)(2,1)}, bf16[1,576,768]{2,1,0:T(8,128)(2,1)S(1)}, u32[]{:S(2)}, u32[]{:S(2)}) collective-permute-start(bf16[1,576,768]{2,1,0:T(8,128)(2,1)} %get-tuple-element.134), channel_id=1, source_target_pairs={{0,16},{8,24},{16,0},{24,8},{1,17},{9,25},{17,1},{25,9},{2,18},{10... | collective-permute-start | bytes 2654216 | tf_op jit(solution)/shard_map/ppermute | solution.py:462
  176.2 46.2 %all-to-all-start.4 = ((bf16[8,40,1152]{2,1,0:T(8,128)(2,1)}), bf16[8,40,1152]{2,1,0:T(8,128)(2,1)S(1)}, u32[]{:S(2)}, u32[]{:S(2)}) async-start(bf16[8,40,1152]{2,1,0:T(8,128)(2,1)} %split.3.refs_18_), calls=%async_computation.4 | async-start | bytes 1474560 | tf_op jit(solution)/shard_map/all_to_all | solution.py:545
  181.5 34.0 %collective-permute-start.18 = (bf16[8,72,768]{2,1,0:T(8,128)(2,1)}, bf16[8,72,768]{2,1,0:T(8,128)(2,1)S(1)}, u32[]{:S(2)}, u32[]{:S(2)}) collective-permute-start(bf16[8,72,768]{2,1,0:T(8,128)(2,1)} %get-tuple-element.135), channel_id=1, source_target_pairs={{0,2},{1,3},{2,0},{3,1},{4,6},{5,7},{6,4},{7,5},{8,10},{9,11},{10,... | collective-permute-start | bytes 2654216 | tf_op jit(solution)/shard_map/ppermute | solution.py:462
  197.9 22.2 %collective-permute-start.11 = (bf16[288,1152]{1,0:T(8,128)(2,1)S(1)}, bf16[288,1152]{1,0:T(8,128)(2,1)S(1)}, u32[]{:S(2)}, u32[]{:S(2)}) collective-permute-start(bf16[288,1152]{1,0:T(8,128)(2,1)S(1)} %copy-done.31), channel_id=1, source_target_pairs={{0,1},{1,0},{2,3},{3,2},{4,5},{5,4},{6,7},{7,6},{8,9},{9,8},{10,11... | collective-permute-start | bytes 1990664 | tf_op jit(solution)/shard_map/ppermute | solution.py:462
  198.0 22.6 %collective-permute-start.12 = (bf16[288,1152]{1,0:T(8,128)(2,1)}, bf16[288,1152]{1,0:T(8,128)(2,1)S(1)}, u32[]{:S(2)}, u32[]{:S(2)}) collective-permute-start(bf16[288,1152]{1,0:T(8,128)(2,1)} %get-tuple-element.127.refs_6_), channel_id=1, source_target_pairs={{0,1},{1,0},{2,3},{3,2},{4,5},{5,4},{6,7},{7,6},{8,9},{9,8},{10,11... | collective-permute-start | bytes 1990664 | tf_op jit(solution)/shard_map/ppermute | solution.py:462
  198.4 22.5 %collective-permute-start.13 = (bf16[288,1152]{1,0:T(8,128)(2,1)}, bf16[288,1152]{1,0:T(8,128)(2,1)S(1)}, u32[]{:S(2)}, u32[]{:S(2)}) collective-permute-start(bf16[288,1152]{1,0:T(8,128)(2,1)} %get-tuple-element.128.refs_7_), channel_id=1, source_target_pairs={{0,1},{1,0},{2,3},{3,2},{4,5},{5,4},{6,7},{7,6},{8,9},{9,8},{10,11... | collective-permute-start | bytes 1990664 | tf_op jit(solution)/shard_map/ppermute | solution.py:462
  198.5 23.8 %collective-permute-start.14 = (bf16[288,1152]{1,0:T(8,128)(2,1)}, bf16[288,1152]{1,0:T(8,128)(2,1)}, u32[]{:S(2)}, u32[]{:S(2)}) collective-permute-start(bf16[288,1152]{1,0:T(8,128)(2,1)} %get-tuple-element.129.refs_8_), channel_id=1, source_target_pairs={{0,1},{1,0},{2,3},{3,2},{4,5},{5,4},{6,7},{7,6},{8,9},{9,8},{10,11... | collective-permute-start | bytes 1990664 | tf_op jit(solution)/shard_map/ppermute | solution.py:462
  215.5 6.8 %collective-permute-start.15 = (bf16[288,1152]{1,0:T(8,128)(2,1)}, bf16[288,1152]{1,0:T(8,128)(2,1)}, u32[]{:S(2)}, u32[]{:S(2)}) collective-permute-start(bf16[288,1152]{1,0:T(8,128)(2,1)} %get-tuple-element.130.refs_9_), channel_id=1, source_target_pairs={{0,1},{1,0},{2,3},{3,2},{4,5},{5,4},{6,7},{7,6},{8,9},{9,8},{10,11... | collective-permute-start | bytes 1990664 | tf_op jit(solution)/shard_map/ppermute | solution.py:462
  220.1 21.5 %collective-permute-start.22 = (bf16[1,288,768]{2,1,0:T(8,128)(2,1)}, bf16[1,288,768]{2,1,0:T(8,128)(2,1)S(1)}, u32[]{:S(2)}, u32[]{:S(2)}) collective-permute-start(bf16[1,288,768]{2,1,0:T(8,128)(2,1)} %get-tuple-element.147), channel_id=1, source_target_pairs={{0,16},{8,24},{16,0},{24,8},{1,17},{9,25},{17,1},{25,9},{2,18},{10... | collective-permute-start | bytes 1327112 | tf_op jit(solution)/shard_map/ppermute | solution.py:462
  220.6 22.6 %collective-permute-start.23 = (bf16[4,72,768]{2,1,0:T(8,128)(2,1)}, bf16[4,72,768]{2,1,0:T(8,128)(2,1)S(1)}, u32[]{:S(2)}, u32[]{:S(2)}) collective-permute-start(bf16[4,72,768]{2,1,0:T(8,128)(2,1)} %get-tuple-element.148), channel_id=1, source_target_pairs={{0,2},{1,3},{2,0},{3,1},{4,6},{5,7},{6,4},{7,5},{8,10},{9,11},{10,... | collective-permute-start | bytes 1327112 | tf_op jit(solution)/shard_map/ppermute | solution.py:462
  221.8 21.4 %collective-permute-start.24 = (bf16[2,144,768]{2,1,0:T(8,128)(2,1)}, bf16[2,144,768]{2,1,0:T(8,128)(2,1)S(1)}, u32[]{:S(2)}, u32[]{:S(2)}) collective-permute-start(bf16[2,144,768]{2,1,0:T(8,128)(2,1)} %get-tuple-element.149), channel_id=1, source_target_pairs={{0,8},{8,0},{16,24},{24,16},{1,9},{9,1},{17,25},{25,17},{2,10},{10... | collective-permute-start | bytes 1327112 | tf_op jit(solution)/shard_map/ppermute | solution.py:462
  238.5 27.5 %collective-permute-start.19 = (bf16[2,288,768]{2,1,0:T(8,128)(2,1)}, bf16[2,288,768]{2,1,0:T(8,128)(2,1)S(1)}, u32[]{:S(2)}, u32[]{:S(2)}) collective-permute-start(bf16[2,288,768]{2,1,0:T(8,128)(2,1)} %get-tuple-element.140), channel_id=1, source_target_pairs={{0,8},{8,0},{16,24},{24,16},{1,9},{9,1},{17,25},{25,17},{2,10},{10... | collective-permute-start | bytes 2654216 | tf_op jit(solution)/shard_map/ppermute | solution.py:462
  240.0 25.9 %collective-permute-start.20 = (bf16[1,576,768]{2,1,0:T(8,128)(2,1)}, bf16[1,576,768]{2,1,0:T(8,128)(2,1)S(1)}, u32[]{:S(2)}, u32[]{:S(2)}) collective-permute-start(bf16[1,576,768]{2,1,0:T(8,128)(2,1)} %get-tuple-element.141), channel_id=1, source_target_pairs={{0,16},{8,24},{16,0},{24,8},{1,17},{9,25},{17,1},{25,9},{2,18},{10... | collective-permute-start | bytes 2654216 | tf_op jit(solution)/shard_map/ppermute | solution.py:462
  241.6 24.4 %collective-permute-start.21 = (bf16[8,72,768]{2,1,0:T(8,128)(2,1)}, bf16[8,72,768]{2,1,0:T(8,128)(2,1)S(1)}, u32[]{:S(2)}, u32[]{:S(2)}) collective-permute-start(bf16[8,72,768]{2,1,0:T(8,128)(2,1)} %get-tuple-element.142), channel_id=1, source_target_pairs={{0,2},{1,3},{2,0},{3,1},{4,6},{5,7},{6,4},{7,5},{8,10},{9,11},{10,... | collective-permute-start | bytes 2654216 | tf_op jit(solution)/shard_map/ppermute | solution.py:462
  246.0 26.7 %collective-permute-start.35 = (bf16[2,72,768]{2,1,0:T(8,128)(2,1)S(1)}, bf16[2,72,768]{2,1,0:T(8,128)(2,1)S(1)}, u32[]{:S(2)}, u32[]{:S(2)}) collective-permute-start(bf16[2,72,768]{2,1,0:T(8,128)(2,1)S(1)} %get-tuple-element.175), channel_id=1, source_target_pairs={{0,2},{1,3},{2,0},{3,1},{4,6},{5,7},{6,4},{7,5},{8,10},{9,11},{10,... | collective-permute-start | bytes 663560 | tf_op jit(solution)/shard_map/ppermute | solution.py:462
  268.5 20.3 %collective-permute-start.25 = (bf16[1,288,768]{2,1,0:T(8,128)(2,1)S(1)}, bf16[1,288,768]{2,1,0:T(8,128)(2,1)S(1)}, u32[]{:S(2)}, u32[]{:S(2)}) collective-permute-start(bf16[1,288,768]{2,1,0:T(8,128)(2,1)S(1)} %get-tuple-element.154), channel_id=1, source_target_pairs={{0,16},{8,24},{16,0},{24,8},{1,17},{9,25},{17,1},{25,9},{2,18},{10... | collective-permute-start | bytes 1327112 | tf_op jit(solution)/shard_map/ppermute | solution.py:462
  269.0 19.8 %collective-permute-start.26 = (bf16[4,72,768]{2,1,0:T(8,128)(2,1)S(1)}, bf16[4,72,768]{2,1,0:T(8,128)(2,1)S(1)}, u32[]{:S(2)}, u32[]{:S(2)}) collective-permute-start(bf16[4,72,768]{2,1,0:T(8,128)(2,1)S(1)} %get-tuple-element.155), channel_id=1, source_target_pairs={{0,2},{1,3},{2,0},{3,1},{4,6},{5,7},{6,4},{7,5},{8,10},{9,11},{10,... | collective-permute-start | bytes 1327112 | tf_op jit(solution)/shard_map/ppermute | solution.py:462
  270.7 18.1 %collective-permute-start.27 = (bf16[2,144,768]{2,1,0:T(8,128)(2,1)S(1)}, bf16[2,144,768]{2,1,0:T(8,128)(2,1)S(1)}, u32[]{:S(2)}, u32[]{:S(2)}) collective-permute-start(bf16[2,144,768]{2,1,0:T(8,128)(2,1)S(1)} %get-tuple-element.156), channel_id=1, source_target_pairs={{0,8},{8,0},{16,24},{24,16},{1,9},{9,1},{17,25},{25,17},{2,10},{10... | collective-permute-start | bytes 1327112 | tf_op jit(solution)/shard_map/ppermute | solution.py:462
  271.2 14.3 %collective-permute-start.36 = (bf16[1,144,768]{2,1,0:T(8,128)(2,1)S(1)}, bf16[1,144,768]{2,1,0:T(8,128)(2,1)S(1)}, u32[]{:S(2)}, u32[]{:S(2)}) collective-permute-start(bf16[1,144,768]{2,1,0:T(8,128)(2,1)S(1)} %get-tuple-element.176), channel_id=1, source_target_pairs={{0,8},{8,0},{16,24},{24,16},{1,9},{9,1},{17,25},{25,17},{2,10},{10... | collective-permute-start | bytes 663560 | tf_op jit(solution)/shard_map/ppermute | solution.py:462
  272.7 12.8 %collective-permute-start.37 = (bf16[1,144,768]{2,1,0:T(8,128)(2,1)S(1)}, bf16[1,144,768]{2,1,0:T(8,128)(2,1)S(1)}, u32[]{:S(2)}, u32[]{:S(2)}) collective-permute-start(bf16[1,144,768]{2,1,0:T(8,128)(2,1)S(1)} %get-tuple-element.177), channel_id=1, source_target_pairs={{0,16},{8,24},{16,0},{24,8},{1,17},{9,25},{17,1},{25,9},{2,18},{10... | collective-permute-start | bytes 663560 | tf_op jit(solution)/shard_map/ppermute | solution.py:462
  286.3 8.5 %collective-permute-start.38 = (bf16[1,72,768]{2,1,0:T(8,128)(2,1)S(1)}, bf16[1,72,768]{2,1,0:T(8,128)(2,1)S(1)}, u32[]{:S(2)}, u32[]{:S(2)}) collective-permute-start(bf16[1,72,768]{2,1,0:T(8,128)(2,1)S(1)} %get-tuple-element.181), channel_id=1, source_target_pairs={{0,4},{1,5},{2,6},{3,7},{4,0},{5,1},{6,2},{7,3},{8,12},{9,13},{10,... | collective-permute-start | bytes 331784 | tf_op jit(solution)/shard_map/ppermute | solution.py:462
  289.8 13.6 %collective-permute-start.28 = (bf16[2,72,768]{2,1,0:T(8,128)(2,1)S(1)}, bf16[2,72,768]{2,1,0:T(8,128)(2,1)S(1)}, u32[]{:S(2)}, u32[]{:S(2)}) collective-permute-start(bf16[2,72,768]{2,1,0:T(8,128)(2,1)S(1)} %get-tuple-element.160), channel_id=1, source_target_pairs={{0,2},{1,3},{2,0},{3,1},{4,6},{5,7},{6,4},{7,5},{8,10},{9,11},{10,... | collective-permute-start | bytes 663560 | tf_op jit(solution)/shard_map/ppermute | solution.py:462
  290.4 13.0 %collective-permute-start.29 = (bf16[1,144,768]{2,1,0:T(8,128)(2,1)S(1)}, bf16[1,144,768]{2,1,0:T(8,128)(2,1)S(1)}, u32[]{:S(2)}, u32[]{:S(2)}) collective-permute-start(bf16[1,144,768]{2,1,0:T(8,128)(2,1)S(1)} %get-tuple-element.161), channel_id=1, source_target_pairs={{0,8},{8,0},{16,24},{24,16},{1,9},{9,1},{17,25},{25,17},{2,10},{10... | collective-permute-start | bytes 663560 | tf_op jit(solution)/shard_map/ppermute | solution.py:462
  291.0 12.5 %collective-permute-start.30 = (bf16[1,144,768]{2,1,0:T(8,128)(2,1)S(1)}, bf16[1,144,768]{2,1,0:T(8,128)(2,1)S(1)}, u32[]{:S(2)}, u32[]{:S(2)}) collective-permute-start(bf16[1,144,768]{2,1,0:T(8,128)(2,1)S(1)} %get-tuple-element.162), channel_id=1, source_target_pairs={{0,16},{8,24},{16,0},{24,8},{1,17},{9,25},{17,1},{25,9},{2,18},{10... | collective-permute-start | bytes 663560 | tf_op jit(solution)/shard_map/ppermute | solution.py:462
  292.5 7.8 %collective-permute-start.39 = (bf16[1,72,768]{2,1,0:T(8,128)(2,1)S(1)}, bf16[1,72,768]{2,1,0:T(8,128)(2,1)S(1)}, u32[]{:S(2)}, u32[]{:S(2)}) collective-permute-start(bf16[1,72,768]{2,1,0:T(8,128)(2,1)S(1)} %get-tuple-element.182), channel_id=1, source_target_pairs={{0,4},{1,5},{2,6},{3,7},{4,0},{5,1},{6,2},{7,3},{8,12},{9,13},{10,... | collective-permute-start | bytes 331784 | tf_op jit(solution)/shard_map/ppermute | solution.py:462
  294.8 7.8 %collective-permute-start.40 = (bf16[1,72,768]{2,1,0:T(8,128)(2,1)S(1)}, bf16[1,72,768]{2,1,0:T(8,128)(2,1)S(1)}, u32[]{:S(2)}, u32[]{:S(2)}) collective-permute-start(bf16[1,72,768]{2,1,0:T(8,128)(2,1)S(1)} %get-tuple-element.183), channel_id=1, source_target_pairs={{0,4},{1,5},{2,6},{3,7},{4,0},{5,1},{6,2},{7,3},{8,12},{9,13},{10,... | collective-permute-start | bytes 331784 | tf_op jit(solution)/shard_map/ppermute | solution.py:462
  303.4 5.2 %collective-permute-start.41 = (bf16[36,2304]{1,0:T(8,128)(2,1)S(1)}, bf16[36,2304]{1,0:T(8,128)(2,1)S(1)}, u32[]{:S(2)}, u32[]{:S(2)}) collective-permute-start(bf16[36,2304]{1,0:T(8,128)(2,1)S(1)} %get-tuple-element.185), channel_id=1, source_target_pairs={{0,1},{1,0},{2,3},{3,2},{4,5},{5,4},{6,7},{7,6},{8,9},{9,8},{10,11... | collective-permute-start | bytes 497672 | tf_op jit(solution)/shard_map/ppermute | solution.py:462
  304.3 13.3 %collective-permute-start.31 = (bf16[1,72,768]{2,1,0:T(8,128)(2,1)S(1)}, bf16[1,72,768]{2,1,0:T(8,128)(2,1)S(1)}, u32[]{:S(2)}, u32[]{:S(2)}) collective-permute-start(bf16[1,72,768]{2,1,0:T(8,128)(2,1)S(1)} %get-tuple-element.166), channel_id=1, source_target_pairs={{0,4},{1,5},{2,6},{3,7},{4,0},{5,1},{6,2},{7,3},{8,12},{9,13},{10,... | collective-permute-start | bytes 331784 | tf_op jit(solution)/shard_map/ppermute | solution.py:462
  304.3 15.6 %collective-permute-start.32 = (bf16[1,72,768]{2,1,0:T(8,128)(2,1)S(1)}, bf16[1,72,768]{2,1,0:T(8,128)(2,1)S(1)}, u32[]{:S(2)}, u32[]{:S(2)}) collective-permute-start(bf16[1,72,768]{2,1,0:T(8,128)(2,1)S(1)} %get-tuple-element.167), channel_id=1, source_target_pairs={{0,4},{1,5},{2,6},{3,7},{4,0},{5,1},{6,2},{7,3},{8,12},{9,13},{10,... | collective-permute-start | bytes 331784 | tf_op jit(solution)/shard_map/ppermute | solution.py:462
  307.3 15.1 %collective-permute-start.33 = (bf16[1,72,768]{2,1,0:T(8,128)(2,1)S(1)}, bf16[1,72,768]{2,1,0:T(8,128)(2,1)S(1)}, u32[]{:S(2)}, u32[]{:S(2)}) collective-permute-start(bf16[1,72,768]{2,1,0:T(8,128)(2,1)S(1)} %get-tuple-element.168), channel_id=1, source_target_pairs={{0,4},{1,5},{2,6},{3,7},{4,0},{5,1},{6,2},{7,3},{8,12},{9,13},{10,... | collective-permute-start | bytes 331784 | tf_op jit(solution)/shard_map/ppermute | solution.py:462
  323.0 2.4 collective-permute-start.34
  (39 other events, 315.3 us)
